TPU v7x, 32 devices: a whole 2x2x4 slice. The times are simulated.
32 devices in a mesh: dp: 8 (over y, x, core), seq: 4 (over z).
Axes of the slice: x: 2, y: 2, z: 4, core: 2. Of those that a mesh axis runs over, the one named last changes fastest.
Arguments:
- audio: float32 [8, 163840], P(None, ('dp', 'seq')), may hold values from -0.4 to 0.4
- starts: int32 [8], replicated, may hold values from 0 to 81919, as said below
- lengths: int32 [8], replicated, may hold values from 40960 to 163840, as said below
- slots: int32 [8], replicated, may hold values from 0 to 7, each once
- conv1_weight: bfloat16 [9, 256], replicated, may hold values from -2 to 2
- conv2_weight: bfloat16 [2304, 256], replicated, may hold values from -0.125 to 0.125
- proj_weight: bfloat16 [5120, 1024], P('dp'), may hold values from -0.078125 to 0.078125
- qkv_weight: bfloat16 [1024, 3072], P('dp'), may hold values from -8 to 8
- out_weight: bfloat16 [1024, 1024], P(None, 'dp'), may hold values from -0.1875 to 0.1875
Outputs:
- regrouped: bfloat16 [8, 8, 4, 8, 1024], P('dp', None, 'seq')
- attended: bfloat16 [8, 8, 4, 8, 1024], P('dp', None, 'seq')
Inputs may be any that keep to these rules, and one draw needn't show every extreme that they name: starts plus lengths is at most 163840 for every stream; some stream's utterance covers the whole stream, and some other stream's utterance starts at 81919. `lengths`: some stream's utterance has exactly 40960 samples. `slots`: every row number appears once.
All inputs are finite; a program needn't handle non-finite values.
Results may differ from a plain program's by a relative error of at most 0.013.
Values may be sent and summed in bfloat16 or wider, within the bound.
No kernel may reach another device: no remote copies, remote signals or barrier semaphores. Data moves between devices by JAX's collectives and lax.ppermute only.
A program may use at most 128 MiB of HBM per device.

v0:
```python
import functools
import math

import jax
import jax.numpy as jnp
import numpy as np
from jax import lax
from jax.experimental import pallas as pl
from jax.experimental.pallas import tpu as pltpu
from jax.sharding import PartitionSpec as P

HEADS = 8
HEAD_DIM = 128
MELS = 80
BANDS = MELS // 4
N_FFT = 512
HOP = 160
W = 8
RIM = 384
SPAN = 4 * HOP
JS = W + 1
LANES = 128
SAMPLE_RATE = 16000.0
EPS_LOG = 1e-06
EPS_NORM = 1e-05
MASKED = -1e30
F32 = jnp.float32
BF16 = jnp.bfloat16
MIB = 1 << 20


def mel_table(size, bands):
    count = size // 2 + 1
    highest = 2595.0 * math.log10(1.0 + SAMPLE_RATE / 1400.0)
    points = np.linspace(0.0, highest, bands + 2)
    edges = 700.0 * (10.0 ** (points / 2595.0) - 1.0)
    edges[0] = 0.0
    edges[-1] = SAMPLE_RATE / 2.0
    frequency = np.arange(count) * (SAMPLE_RATE / size)
    lower = edges[:-2][None, :]
    middle = edges[1:-1][None, :]
    upper = edges[2:][None, :]
    rising = (frequency[:, None] - lower) / (middle - lower)
    falling = (upper - frequency[:, None]) / (upper - middle)
    return np.maximum(0.0, np.minimum(rising, falling)).astype(np.float32)


def filter_table():
    table = mel_table(N_FFT, MELS)[: N_FFT // 2]
    return np.pad(table, ((0, 0), (0, LANES - MELS)))


def spectrum_table(size):
    sample = np.arange(size)
    phase = sample[:, None] * np.arange(size // 2)[None, :] % size
    angle = phase * (2.0 * math.pi / size)
    window = 0.5 - 0.5 * np.cos(sample * (2.0 * math.pi / size))
    both = np.concatenate([np.cos(angle), np.sin(angle)], axis=1) * window[:, None]
    return both.astype(np.float32)


def band_selection(parts):
    share = BANDS // parts
    width = 4 * share + 4
    table = np.zeros((4 * LANES, parts * LANES), np.float32)
    for part in range(parts):
        for delta in range(4):
            for lane in range(width):
                band = 4 * share * part - 4 + lane
                if 0 <= band < MELS:
                    table[delta * LANES + band, part * LANES + delta * width + lane] = 1.0
    return table.astype(BF16)


def shift_selection(width):
    table = np.zeros((LANES, 2 * LANES), np.float32)
    lane = np.arange(width)
    for delta in range(3):
        table[(delta + 1) * width + lane, delta * width + lane] = 1.0
    for delta in range(2):
        table[delta * width + lane, LANES + (delta + 3) * width + lane] = 1.0
    return table.astype(BF16)


def row_selection(windows, group):
    count = windows * group
    earlier = np.zeros((JS * count, W * count), np.float32)
    same = np.zeros((JS * count, W * count), np.float32)
    for j in range(JS):
        for s in range(group):
            for k in range(windows):
                row = j * count + s * windows + k
                window = k * group + s
                if j:
                    earlier[row, window * W + j - 1] = 1.0
                elif window:
                    earlier[row, (window - 1) * W + W - 1] = 1.0
                if j < W:
                    same[row, window * W + j] = 1.0
    return np.concatenate([earlier, same], axis=1).astype(BF16)


def frame_table(windows):
    count = windows * W
    table = np.zeros((count, count), np.float32)
    for k in range(windows):
        for t in range(W):
            table[k * W + t, t * windows + k] = 1.0
    return table.astype(BF16)


def vmem():
    return pl.BlockSpec(memory_space=pltpu.VMEM)


def smem():
    return pl.BlockSpec(memory_space=pltpu.SMEM)


def anywhere():
    return pl.BlockSpec(memory_space=pl.ANY)


def hbm():
    return pl.BlockSpec(memory_space=pltpu.HBM)


def params(mib):
    return pltpu.CompilerParams(vmem_limit_bytes=mib * MIB)


def cost(flops, moved):
    return pl.CostEstimate(flops=int(flops), bytes_accessed=int(moved), transcendentals=0)


def place(parts):
    mine = lax.axis_index("dp")
    copies = lax.axis_size("dp") // parts
    return mine // copies, mine % copies


def later(index, step, count):
    return lax.rem(index + step, count)


def start_all(copies):
    for copy in copies:
        copy.start()


def wait_all(copies):
    for copy in copies:
        copy.wait()


def loads_of(sources, targets, sems, base):
    return [
        pltpu.make_async_copy(source, target, sems.at[base + i])
        for i, (source, target) in enumerate(zip(sources, targets))
    ]


def prep_kernel(parts, width, tables, conv1_ref, qkv_ref, out_ref, *refs):
    table_refs, refs = refs[:tables], refs[tables:]
    table_outs, refs = refs[:tables], refs[tables:]
    pack_outs, (banded_out, sems) = refs[:parts], refs[parts:]
    part, _ = place(parts)
    rows = qkv_ref.shape[0]
    features = qkv_ref.shape[1] // 3
    head_width = features // parts
    blocks = head_width // LANES
    copies = loads_of(table_refs, table_outs, sems, 0)
    for step in range(parts):
        first = pl.multiple_of(later(part, step, parts) * head_width, LANES)
        for kind in range(3):
            for piece in range(blocks):
                source = qkv_ref.at[:, pl.ds(kind * features + first + piece * LANES, LANES)]
                target = pack_outs[step].at[pl.ds((kind * blocks + piece) * rows, rows)]
                copies.append(pltpu.make_async_copy(source, target, sems.at[len(copies)]))
        target = pack_outs[step].at[pl.ds(3 * blocks * rows, out_ref.shape[0])]
        copies.append(pltpu.make_async_copy(out_ref, target, sems.at[len(copies)]))
    start_all(copies)
    taps, channels = conv1_ref.shape
    outs = banded_out.shape[1] // channels
    row = lax.broadcasted_iota(jnp.int32, (LANES, taps), 0)
    tap = lax.broadcasted_iota(jnp.int32, (LANES, taps), 1)
    line = (tap >= 3).astype(jnp.int32) + (tap >= 6).astype(jnp.int32)
    target = line * (width - 3) + tap + 1
    weight = conv1_ref[...]
    for g in range(outs):
        select = (row == target + 2 * g).astype(F32).astype(BF16)
        banded_out[:, g * channels : (g + 1) * channels] = jnp.dot(
            select, weight, preferred_element_type=F32
        ).astype(BF16)
    wait_all(copies)


def mel_kernel(
    parts, group, tables, slots_ref, rim_ref, audio_ref, table_ref, filter_ref, select_ref, *refs
):
    table_refs, refs = refs[:tables], refs[tables:]
    out_ref, refs = refs[0], refs[1:]
    table_outs, (ext, sems) = refs[:tables], refs[tables:]
    loads = loads_of(table_refs, table_outs, sems, 0)
    start_all(loads)
    streams = audio_ref.shape[0]
    rows = W * streams
    ext[:, :RIM] = rim_ref[...]
    ext[:, RIM:] = audio_ref[...]
    phases = []
    for phase in range(4):
        start = HOP * phase + 32
        base, shift = start // LANES * LANES, start % LANES
        length = N_FFT + (LANES if shift else 0)
        block = jnp.concatenate(
            [ext[:, SPAN * j + base : SPAN * j + base + length] for j in range(W)], axis=0
        )
        if shift:
            block = pltpu.roll(block, length - shift, 1)[:, :N_FFT]
        phases.append(block)
    frames = jnp.concatenate(phases, axis=0)
    spectrum = jnp.dot(frames, table_ref[...], precision=lax.Precision.HIGHEST, preferred_element_type=F32)
    half = N_FFT // 2
    real, imag = spectrum[:, :half], spectrum[:, half:]
    power = real * real + imag * imag
    mel_power = jnp.dot(power, filter_ref[...], precision=lax.Precision.HIGHEST, preferred_element_type=F32)
    log_mel = jnp.log(mel_power + EPS_LOG).astype(BF16)
    gathered = jnp.concatenate([log_mel[phase * rows : (phase + 1) * rows] for phase in range(4)], axis=1)
    placed = jnp.dot(gathered, select_ref[...], preferred_element_type=F32).astype(BF16)
    column = lax.broadcasted_iota(jnp.int32, (1, rows), 1)
    early = jnp.zeros((1, rows), jnp.int32)
    for j in range(1, W):
        early += (column >= j * streams).astype(jnp.int32)
    target = jnp.zeros((1, rows), jnp.int32)
    for u in range(streams):
        target = jnp.where(column - early * streams == u, slots_ref[u] * W + early, target)
    routing = (target == lax.broadcasted_iota(jnp.int32, (rows, rows), 0)).astype(F32).astype(BF16)
    routed = jnp.dot(routing, placed, preferred_element_type=F32)
    copies = streams // group
    for part in range(parts):
        for copy in range(copies):
            for plane in range(group):
                row = plane * copies + copy
                out_ref[(part * copies + copy) * group + plane] = routed[
                    row * W : (row + 1) * W, part * LANES : (part + 1) * LANES
                ].astype(BF16)
    wait_all(loads)


def conv_kernel(parts, width, windows, mel_ref, banded_ref, conv2, rows_ref, shift_ref, *refs):
    part, copy_index = place(parts)
    copies = lax.axis_size("dp") // parts
    proj_refs, refs = refs[:copies], refs[copies:]
    pack_refs, refs = refs[:parts], refs[parts:]
    outs_refs, refs = refs[:parts], refs[parts:]
    stack_out, even, odd, second, proj, partial, sems = refs
    loads = []
    for step in range(copies):
        slot = later(copy_index, copies - step, copies)
        loads.append(pltpu.make_async_copy(proj_refs[step], proj.at[slot], sems.at[step]))
    for step in range(parts):
        slot = later(part, parts - step, parts)
        loads.append(pltpu.make_async_copy(pack_refs[step], stack_out.at[slot], sems.at[copies + step]))
    start_all(loads)
    sources = mel_ref.shape[0]
    n = sources
    payload = mel_ref[...].astype(F32).reshape(sources * W, LANES).astype(BF16)
    shifted = jnp.dot(payload, shift_ref[...], preferred_element_type=F32).astype(BF16)
    both = jnp.concatenate([shifted[:, :LANES], shifted[:, LANES:]], axis=0)
    evens = jnp.dot(rows_ref[...], both, preferred_element_type=F32)
    row = lax.broadcasted_iota(jnp.int32, evens.shape, 0)
    lane = lax.broadcasted_iota(jnp.int32, evens.shape, 1)
    low = (lane >= width).astype(jnp.int32) + (lane >= 2 * width).astype(jnp.int32)
    band = lane - low * width - 4 + (width - 4) * part
    silent = (row == 0) & (lane < 3 * width) & (band >= 0)
    evens = jnp.where(silent, jnp.log(jnp.full(evens.shape, EPS_LOG, F32)), evens)
    odds = pltpu.roll(evens[: W * n], LANES - 2 * width, 1).astype(BF16)
    evens = evens.astype(BF16)
    channels = conv2.shape[1]
    outs = banded_ref.shape[1] // channels
    for g in range(outs):
        lanes = slice(g * channels, (g + 1) * channels)
        weight = banded_ref[:, lanes]
        even[:, lanes] = jax.nn.relu(jnp.dot(evens, weight, preferred_element_type=F32)).astype(BF16)
        odd[:, lanes] = jax.nn.relu(jnp.dot(odds, weight, preferred_element_type=F32)).astype(BF16)

    for h in range((outs - 1) // 2):
        lanes = slice(2 * h * channels, (2 * h + 3) * channels)
        depth = 3 * channels
        total = jnp.dot(even[: W * n, lanes], conv2[:depth], preferred_element_type=F32)
        total += jnp.dot(odd[:, lanes], conv2[depth : 2 * depth], preferred_element_type=F32)
        total += jnp.dot(even[n:, lanes], conv2[2 * depth :], preferred_element_type=F32)
        second[:, h * channels : (h + 1) * channels] = jax.nn.relu(total).astype(BF16)
    wait_all(loads)
    weights = proj[...].reshape(second.shape[1], proj.shape[2])
    partial[...] = jnp.dot(second[...], weights, preferred_element_type=F32)
    for step in range(parts):
        plane = later(part, step, parts)
        outs_refs[step][...] = jnp.concatenate(
            [partial[pl.ds(pl.multiple_of(t * n + plane * windows, 8), windows), :] for t in range(W)], axis=0
        ).astype(BF16)


def bounds(row, slots_ref, starts_ref, lengths_ref):
    begin, span = jnp.int32(0), jnp.int32(0)
    for u in range(slots_ref.shape[0]):
        chosen = slots_ref[u] == row
        begin = begin + jnp.where(chosen, starts_ref[u], 0)
        span = span + jnp.where(chosen, lengths_ref[u], 0)
    return begin, begin + span


def place_mix(parts, rows, stack_refs, buffer, sems, base):
    _, copy_index = place(parts)
    copies = len(stack_refs)
    moves = []
    for step in range(copies):
        slot = later(copy_index, copies - step, copies)
        for piece in range(parts):
            for block in range(buffer.shape[2] // LANES):
                source = stack_refs[step].at[piece, pl.ds(block * rows, rows)]
                target = buffer.at[piece * copies + slot, :, pl.ds(block * LANES, LANES)]
                moves.append(pltpu.make_async_copy(source, target, sems.at[base + len(moves)]))
    return moves


def place_out(parts, rows, stack_refs, buffer, sems, base):
    _, copy_index = place(parts)
    copies = len(stack_refs)
    moves = []
    for step in range(copies):
        slot = later(copy_index, copies - step, copies)
        for piece in range(parts):
            source = stack_refs[step].at[piece, pl.ds(rows, buffer.shape[1])]
            target = buffer.at[piece * copies + slot]
            moves.append(pltpu.make_async_copy(source, target, sems.at[base + len(moves)]))
    return moves


def norm_kernel(parts, slots_ref, starts_ref, lengths_ref, frames_ref, sample_ref, *refs):
    part, copy_index = place(parts)
    copies = lax.axis_size("dp") // parts
    part_refs, refs = refs[:parts], refs[parts:]
    stack_refs, refs = refs[:copies], refs[copies:]
    rows_out, normed_out, mix_out, sems = refs
    moves = place_mix(parts, mix_out.shape[1], stack_refs, mix_out, sems, 0)
    start_all(moves)
    row = lax.axis_index("seq") * copies + copy_index
    begin, end = bounds(row, slots_ref, starts_ref, lengths_ref)
    total = part_refs[0][...].astype(F32)
    for step in range(1, parts):
        total += part_refs[step][...].astype(F32)
    encoded = total.astype(BF16)
    values = encoded.astype(F32)
    mean = jnp.mean(values, axis=-1, keepdims=True)
    centered = values - mean
    variance = jnp.mean(centered * centered, axis=-1, keepdims=True)
    normed_out[...] = (centered * lax.rsqrt(variance + EPS_NORM)).astype(BF16)
    ordered = jnp.dot(frames_ref[...], encoded, preferred_element_type=F32)
    sample = sample_ref[...] + part * (W * SPAN)
    valid = (sample >= begin) & (sample < end)
    rows_out[...] = jnp.where(valid, ordered, 0.0).astype(BF16)
    wait_all(moves)


def attention_kernel(parts, mix_rows, slots_ref, starts_ref, lengths_ref, sample_ref, mix_ref, *refs):
    part, copy_index = place(parts)
    copies = lax.axis_size("dp") // parts
    normed_refs, refs = refs[:parts], refs[parts:]
    stack_refs, refs = refs[:copies], refs[copies:]
    outs_refs, (weights_out, sems) = refs[:parts], refs[parts:]
    moves = place_out(parts, mix_rows, stack_refs, weights_out, sems, 0)
    start_all(moves)
    row = lax.axis_index("seq") * copies + copy_index
    begin, end = bounds(row, slots_ref, starts_ref, lengths_ref)
    masks = []
    for step in range(parts):
        plane = later(part, parts - step, parts)
        sample = sample_ref[...] + plane * (W * SPAN)
        masks.append(((sample >= begin) & (sample < end)).astype(F32))
    valid = jnp.concatenate(masks, axis=1) > 0.5
    normed = jnp.concatenate([ref[...] for ref in normed_refs], axis=0)
    local, features = normed_refs[0].shape
    weights = mix_ref[...].reshape(features, mix_ref.shape[2])
    mixed = jnp.dot(normed, weights, preferred_element_type=F32).astype(BF16)
    width = mix_ref.shape[2] // 3
    scale = HEAD_DIM ** (-0.5)
    for head in range(width // HEAD_DIM):
        at = head * HEAD_DIM
        query = mixed[:, at : at + HEAD_DIM]
        key = mixed[:, width + at : width + at + HEAD_DIM]
        value = mixed[:, 2 * width + at : 2 * width + at + HEAD_DIM]
        scores = lax.dot_general(query, key, (((1,), (1,)), ((), ())), preferred_element_type=F32) * scale
        masked = jnp.where(valid, scores, MASKED)
        peak = jnp.max(masked, axis=1, keepdims=True)
        weight = jnp.where(valid, jnp.exp(masked - peak), 0.0)
        total = jnp.sum(weight, axis=1, keepdims=True)
        summed = jnp.dot(weight.astype(BF16), value, preferred_element_type=F32)
        context = (summed / total).astype(BF16)
        for step in range(parts):
            outs_refs[step][:, at : at + HEAD_DIM] = context[step * local : (step + 1) * local]
    wait_all(moves)


def output_kernel(parts, slots_ref, starts_ref, lengths_ref, frames_ref, sample_ref, weights_ref, rows_ref, *refs):
    context_refs, refs = refs[:parts], refs[parts:]
    rows_out, out_ref, context, sems = refs
    keep = pltpu.make_async_copy(rows_ref, rows_out, sems.at[0])
    keep.start()
    plane = lax.axis_index("seq")
    begin, end = bounds(lax.axis_index("dp"), slots_ref, starts_ref, lengths_ref)
    head_width = context_refs[0].shape[1]
    for step in range(parts):
        at = pl.multiple_of(later(plane, step, parts) * head_width, LANES)
        context[:, pl.ds(at, head_width)] = context_refs[step][...]
    ordered = jnp.dot(frames_ref[...], context[...], preferred_element_type=F32).astype(BF16)
    sample = sample_ref[...] + plane * (W * SPAN)
    valid = (sample >= begin) & (sample < end)
    result = jnp.concatenate(
        [jnp.dot(ordered, weights_ref[d], preferred_element_type=F32) for d in range(weights_ref.shape[0])], axis=1
    )
    out_ref[...] = jnp.where(valid, result, 0.0).astype(BF16)
    keep.wait()


def on_device(
    audio, starts, lengths, slots, conv1_weight, conv2_weight, proj_weight, qkv_weight, out_weight
):
    streams = audio.shape[0]
    windows = lax.axis_size("dp")
    group = lax.axis_size("seq")
    parts = group
    copies = windows // parts
    assert BANDS % parts == 0 and streams == copies * group and streams == windows
    share = BANDS // parts
    width = 4 * share + 4
    channels = conv1_weight.shape[1]
    features = proj_weight.shape[1]
    head_width = features // parts
    local = windows * W
    sources = windows * group
    n = sources
    outs = 2 * share + 1

    route = [(i, i + 1) for i in range(sources - 1)]
    rim = lax.ppermute(audio[:, audio.shape[1] - RIM :], ("dp", "seq"), route)

    def to_part(block, step):
        pairs = [(p * copies + c, (p + step) % parts * copies + c) for p in range(parts) for c in range(copies)]
        return lax.ppermute(block, "dp", pairs)

    def to_copy(block, step):
        pairs = [(p * copies + c, p * copies + (c + step) % copies) for p in range(parts) for c in range(copies)]
        return lax.ppermute(block, "dp", pairs)

    def to_owner(block, step):
        pairs = []
        for p in range(parts):
            for c in range(copies):
                for z in range(group):
                    pairs.append(((p * copies + c) * group + z, (z * copies + c) * group + (p - step) % parts))
        return lax.ppermute(block, ("dp", "seq"), pairs)

    scale = sources // 32
    proj_all = [proj_weight] + [to_copy(proj_weight, step) for step in range(1, copies)]

    def like(array):
        return jax.ShapeDtypeStruct(array.shape, array.dtype)

    tables = [
        audio,
        jnp.asarray(spectrum_table(N_FFT)),
        jnp.asarray(filter_table()),
        jnp.asarray(band_selection(parts)),
    ]
    mix_rows = 3 * head_width // LANES * qkv_weight.shape[0]
    out_packed = out_weight.reshape(-1, LANES)
    pack = jax.ShapeDtypeStruct((mix_rows + out_packed.shape[0], LANES), BF16)
    prepared = pl.pallas_call(
        functools.partial(prep_kernel, parts, width, len(tables)),
        out_shape=tuple(
            [like(table) for table in tables]
            + [pack] * parts
            + [jax.ShapeDtypeStruct((LANES, outs * channels), BF16)]
        ),
        in_specs=[vmem()] + [hbm()] * (2 + len(tables)),
        out_specs=tuple([vmem()] * len(tables) + [anywhere()] * parts + [vmem()]),
        scratch_shapes=[
            pltpu.SemaphoreType.DMA((len(tables) + parts * (3 * head_width // LANES + 1),))
        ],
        compiler_params=params(min(16 * scale, 32)),
        cost_estimate=cost(1e8, 4e6),
        name="prep",
    )(conv1_weight, qkv_weight, out_packed, *tables)
    tables, packs, banded = prepared[: len(tables)], prepared[len(tables) : -1], prepared[-1]

    later_tables = [
        conv2_weight,
        jnp.asarray(row_selection(windows, group)),
        jnp.asarray(shift_selection(width)),
    ]
    mel, *later_tables = pl.pallas_call(
        functools.partial(mel_kernel, parts, group, len(later_tables)),
        out_shape=tuple(
            [jax.ShapeDtypeStruct((sources, W, LANES), BF16)] + [like(table) for table in later_tables]
        ),
        in_specs=[smem()] + [vmem()] * (1 + len(tables)) + [hbm()] * len(later_tables),
        out_specs=tuple([vmem()] * (1 + len(later_tables))),
        scratch_shapes=[
            pltpu.VMEM((streams, RIM + audio.shape[1]), F32),
            pltpu.SemaphoreType.DMA((len(later_tables),)),
        ],
        compiler_params=params(min(20 * scale, 48)),
        cost_estimate=cost(2e9, 2e6),
        name="log_mel",
    )(slots, rim, *tables, *later_tables)
    mel, *packs = lax.optimization_barrier((mel, *packs))
    mel = lax.all_to_all(mel, ("dp", "seq"), split_axis=0, concat_axis=0, tiled=True)
    packs = [packs[0]] + [to_part(packs[step], step) for step in range(1, parts)]

    block = jax.ShapeDtypeStruct((local, features), BF16)
    *partials, stack = pl.pallas_call(
        functools.partial(conv_kernel, parts, width, windows),
        out_shape=tuple([block] * parts + [jax.ShapeDtypeStruct((parts,) + pack.shape, BF16)]),
        in_specs=[vmem()] * (2 + len(later_tables)) + [anywhere()] * (copies + parts),
        out_specs=tuple([vmem()] * parts + [anywhere()]),
        scratch_shapes=[
            pltpu.VMEM((JS * n, banded.shape[1]), BF16),
            pltpu.VMEM((W * n, banded.shape[1]), BF16),
            pltpu.VMEM((W * n, share * channels), BF16),
            pltpu.VMEM((copies,) + proj_weight.shape, BF16),
            pltpu.VMEM((W * n, features), F32),
            pltpu.SemaphoreType.DMA((copies + parts,)),
        ],
        compiler_params=params(min(24 * scale, 48)),
        cost_estimate=cost(8e9, 4e6),
        name="conv",
    )(mel, banded, *later_tables, *proj_all, *packs)
    stacks = [stack] + [to_copy(stack, step) for step in range(1, copies)]
    partials = [partials[0]] + [to_part(partials[step], step) for step in range(1, parts)]

    index = np.arange(local)
    out_sample = ((index // W) * group * W + index % W) * SPAN
    key_sample = ((index % windows) * group * W + index // windows) * SPAN
    out_sample = jnp.asarray(out_sample.reshape(-1, 1).astype(np.int32))
    key_sample = jnp.asarray(key_sample.reshape(1, -1).astype(np.int32))
    frames = jnp.asarray(frame_table(windows))
    mix = jax.ShapeDtypeStruct((windows, qkv_weight.shape[0], 3 * head_width), BF16)
    regrouped, normed, mix = pl.pallas_call(
        functools.partial(norm_kernel, parts),
        out_shape=(block, block, mix),
        in_specs=[smem()] * 3 + [vmem()] * (2 + parts) + [anywhere()] * copies,
        out_specs=(vmem(), vmem(), vmem()),
        scratch_shapes=[pltpu.SemaphoreType.DMA((windows * (3 * head_width // LANES),))],
        compiler_params=params(min(12 * scale, 32)),
        cost_estimate=cost(1e8, 1e6),
        name="layer_norm",
    )(slots, starts, lengths, frames, out_sample, *partials, *stacks)
    normed = [normed] + [to_part(normed, step) for step in range(1, parts)]
    regrouped = to_owner(regrouped, 0)

    out_columns = jax.ShapeDtypeStruct((windows,) + out_weight.shape, BF16)
    if out_packed.shape != out_weight.shape:
        stacks = [stack[:, mix_rows:].reshape((parts,) + out_weight.shape) for stack in stacks]
        mix_rows = 0
    *context, out_columns = pl.pallas_call(
        functools.partial(attention_kernel, parts, mix_rows),
        out_shape=tuple([jax.ShapeDtypeStruct((local, head_width), BF16)] * parts + [out_columns]),
        in_specs=[smem()] * 3 + [vmem()] * (2 + parts) + [anywhere()] * copies,
        out_specs=tuple([vmem()] * (parts + 1)),
        scratch_shapes=[pltpu.SemaphoreType.DMA((windows,))],
        compiler_params=params(min(16 * scale, 48)),
        cost_estimate=cost(1e9, 2e6),
        name="attention",
    )(slots, starts, lengths, key_sample, mix, *normed, *stacks)
    context = [to_owner(context[step], step) for step in range(parts)]

    regrouped, attended = pl.pallas_call(
        functools.partial(output_kernel, parts),
        out_shape=(block, block),
        in_specs=[smem()] * 3 + [vmem()] * 3 + [anywhere()] + [vmem()] * parts,
        out_specs=(anywhere(), vmem()),
        scratch_shapes=[pltpu.VMEM((local, features), BF16), pltpu.SemaphoreType.DMA((1,))],
        compiler_params=params(min(12 * scale, 32)),
        cost_estimate=cost(1e8, 3e6),
        name="output",
    )(slots, starts, lengths, frames, out_sample, out_columns, regrouped, *context)
    shape = (1, windows, 1, W, features)
    return (regrouped.reshape(shape), attended.reshape(shape))


def solution(mesh):
    in_specs = (
        P(None, ("dp", "seq")),
        P(),
        P(),
        P(),
        P(),
        P(),
        P("dp", None),
        P("dp", None),
        P(None, "dp"),
    )
    out_specs = (P("dp", None, "seq", None, None), P("dp", None, "seq", None, None))
    return jax.shard_map(
        on_device, mesh=mesh, in_specs=in_specs, out_specs=out_specs, check_vma=False
    )
```

profile of v0, /device:TPU:0, one launch (start us, length us, event | category | flops | bytes accessed | tf_op | source)
XLA Modules:
  0.0 86.9 jit_solution(18356972682318348715)
XLA Ops:
  0.6 0.5 collective-permute-start.1
  1.2 0.7 slice.3
  1.9 4.5 %collective-permute-start = (f32[8,384]{1,0:T(8,128)S(1)}, f32[8,384]{1,0:T(8,128)S(1)}, u32[]{:S(2)}, u32[]{:S(2)}) collective-permute-start(f32[8,384]{1,0:T(8,128)S(1)} %slice.3), channel_id=1, source_target_pairs={{0,1},{1,2},{2,3},{3,4},{4,5},{5,6},{6,7},{7,8},{8,9},{9,10},{10,1... | collective-permute-start | bytes 36872 | tf_op jit(solution)/shard_map/ppermute | solution.py:446
  6.4 0.0 copy-start
  6.4 1.2 %copy-done = f32[512,512]{1,0:T(8,128)S(1)} copy-done((f32[512,512]{1,0:T(8,128)S(1)}, f32[512,512]{1,0:T(8,128)}, u32[]{:S(2)}) %copy-start) | copy-done | bytes 1048600
  7.6 1.1 %copy-done.1 = bf16[128,3072]{1,0:T(8,128)(2,1)S(1)} copy-done((bf16[128,3072]{1,0:T(8,128)(2,1)S(1)}, bf16[128,3072]{1,0:T(8,128)(2,1)}, u32[]{:S(2)}) %copy-start.1) | copy-done | bytes 786456
  8.7 1.0 %copy-done.2 = bf16[512,512]{1,0:T(8,128)(2,1)S(1)} copy-done((bf16[512,512]{1,0:T(8,128)(2,1)S(1)}, bf16[512,512]{1,0:T(8,128)(2,1)}, u32[]{:S(2)}) %copy-start.2) | copy-done | bytes 524312
  9.8 0.9 %copy-done.3 = bf16[1024,128]{1,0:T(8,128)(2,1)S(1)} copy-done((bf16[1024,128]{1,0:T(8,128)(2,1)S(1)}, bf16[1024,128]{1,0:T(8,128)(2,1)}, u32[]{:S(2)}) %copy-start.3) | copy-done | bytes 262168
  10.7 0.9 %copy-done.4 = f32[8,5120]{1,0:T(8,128)S(1)} copy-done((f32[8,5120]{1,0:T(8,128)S(1)}, f32[8,5120]{1,0:T(8,128)}, u32[]{:S(2)}) %copy-start.4) | copy-done | bytes 163864
  11.6 0.9 %copy-done.6 = f32[256,128]{1,0:T(8,128)S(1)} copy-done((f32[256,128]{1,0:T(8,128)S(1)}, f32[256,128]{1,0:T(8,128)}, u32[]{:S(2)}) %copy-start.6) | copy-done | bytes 131096
  12.5 0.7 copy-done.8
  13.2 1.5 %prep.1 = (f32[8,5120]{1,0:T(8,128)S(1)}, f32[512,512]{1,0:T(8,128)S(1)}, f32[256,128]{1,0:T(8,128)S(1)}, bf16[512,512]{1,0:T(8,128)(2,1)S(1)}, bf16[1792,128]{1...) custom-call(bf16[9,256]{1,0:T(8,128)(2,1)S(1)} %copy-done.8, ...), custom_call_target="tpu_custom_call" | custom-call | flops 100000000 | bytes 4000000 | tf_op jit(solution)/shard_map/prep/pallas_call | solution.py:479
  14.8 0.0 copy-start.13
  14.8 2.9 %log_mel.1 = (bf16[32,8,128]{2,1,0:T(8,128)(2,1)S(1)}, bf16[2304,256]{1,0:T(8,128)(2,1)S(1)}, bf16[288,512]{1,0:T(8,128)(2,1)S(1)}, bf16[128,256]{1,0:T(8,128)(2,1)S(1)}) custom-call(s32[8]{0:T(128)S(1)} %copy-done.9, f32[8,384]{1,0:T(8,128)S(1)} %collective-permute-done.rim_ref, f32[8,5120]{1,0:T(8,128)S(1)} %get-tuple-element.35.audio_ref, ...), custom_call_target="tpu_custom_call" | custom-call | flops 2000000000 | bytes 2000000 | tf_op jit(solution)/shard_map/log_mel/pallas_call | solution.py:502
  17.7 1.5 %collective-permute-start.2 = (bf16[1792,128]{1,0:T(8,128)(2,1)S(1)}, bf16[1792,128]{1,0:T(8,128)(2,1)S(1)}, u32[]{:S(2)}, u32[]{:S(2)}) collective-permute-start(bf16[1792,128]{1,0:T(8,128)(2,1)S(1)} %get-tuple-element.50), channel_id=1, source_target_pairs={{0,8},{4,12},{8,16},{12,20},{16,24},{20,28},{24,0},{28,4},{1,9},{5... | collective-permute-start | bytes 1376264 | tf_op jit(solution)/shard_map/ppermute | solution.py:450
  19.2 1.5 %collective-permute-start.3 = (bf16[1792,128]{1,0:T(8,128)(2,1)S(1)}, bf16[1792,128]{1,0:T(8,128)(2,1)S(1)}, u32[]{:S(2)}, u32[]{:S(2)}) collective-permute-start(bf16[1792,128]{1,0:T(8,128)(2,1)S(1)} %get-tuple-element.51), channel_id=1, source_target_pairs={{0,16},{4,20},{8,24},{12,28},{16,0},{20,4},{24,8},{28,12},{1,17},{... | collective-permute-start | bytes 1376264 | tf_op jit(solution)/shard_map/ppermute | solution.py:450
  20.8 1.4 %collective-permute-start.4 = (bf16[1792,128]{1,0:T(8,128)(2,1)S(1)}, bf16[1792,128]{1,0:T(8,128)(2,1)S(1)}, u32[]{:S(2)}, u32[]{:S(2)}) collective-permute-start(bf16[1792,128]{1,0:T(8,128)(2,1)S(1)} %get-tuple-element.52), channel_id=1, source_target_pairs={{0,24},{4,28},{8,0},{12,4},{16,8},{20,12},{24,16},{28,20},{1,25},{... | collective-permute-start | bytes 1376264 | tf_op jit(solution)/shard_map/ppermute | solution.py:450
  22.2 19.7 %all_to_all.5.mel_ref = bf16[32,8,128]{2,1,0:T(8,128)(2,1)S(1)} all-to-all(bf16[32,8,128]{2,1,0:T(8,128)(2,1)S(1)} %get-tuple-element.44), channel_id=1, replica_groups=mesh['dp'=8,'seq'=4] {'dp','seq'}, dimensions={0} | all-to-all | bytes 131072 | tf_op jit(solution)/shard_map/all_to_all | solution.py:518
  41.9 0.0 collective-permute-done.1.refs_1_
  41.9 0.0 copy-start.5
  41.9 0.0 copy-start.7
  41.9 0.0 copy-start.10
  41.9 0.0 copy-start.11
  41.9 5.8 %conv.1 = (bf16[64,1024]{1,0:T(8,128)(2,1)S(1)}, bf16[64,1024]{1,0:T(8,128)(2,1)S(1)}, bf16[64,1024]{1,0:T(8,128)(2,1)S(1)}, bf16[64,1024]{1,0:T(8,128)(2,1)S(1)}, bf16[4,1792,128]{2,1,0:T(8,128)(2,1)S(1)}) custom-call(bf16[32,8,128]{2,1,0:T(8,128)(2,1)S(1)} %all_to_all.5.mel_ref, bf16[128,2816]{1,0:T(8,128)(2,1)S(1)} %get-tuple-element.45.banded_ref, ...), custom_call_target="tpu_custom_call" | custom-call | flops 8000000000 | bytes 4000000 | tf_op jit(solution)/shard_map/conv/pallas_call | solution.py:522
  47.7 0.2 collective-permute-start.8
  47.9 1.7 %collective-permute-start.5 = (bf16[64,1024]{1,0:T(8,128)(2,1)S(1)}, bf16[64,1024]{1,0:T(8,128)(2,1)S(1)}, u32[]{:S(2)}, u32[]{:S(2)}) collective-permute-start(bf16[64,1024]{1,0:T(8,128)(2,1)S(1)} %get-tuple-element.54), channel_id=1, source_target_pairs={{0,8},{4,12},{8,16},{12,20},{16,24},{20,28},{24,0},{28,4},{1,9},{5... | collective-permute-start | bytes 393224 | tf_op jit(solution)/shard_map/ppermute | solution.py:450
  49.6 0.5 collective-permute-start.6
  50.2 2.2 %collective-permute-start.7 = (bf16[64,1024]{1,0:T(8,128)(2,1)S(1)}, bf16[64,1024]{1,0:T(8,128)(2,1)S(1)}, u32[]{:S(2)}, u32[]{:S(2)}) collective-permute-start(bf16[64,1024]{1,0:T(8,128)(2,1)S(1)} %get-tuple-element.56), channel_id=1, source_target_pairs={{0,24},{4,28},{8,0},{12,4},{16,8},{20,12},{24,16},{28,20},{1,25},{... | collective-permute-start | bytes 393224 | tf_op jit(solution)/shard_map/ppermute | solution.py:450
  52.3 2.9 %collective-permute-done.5.refs_1_ = bf16[64,1024]{1,0:T(8,128)(2,1)S(1)} collective-permute-done((bf16[64,1024]{1,0:T(8,128)(2,1)S(1)}, bf16[64,1024]{1,0:T(8,128)(2,1)S(1)}, u32[]{:S(2)}, u32[]{:S(2)}) %collective-permute-start.5) | collective-permute-done | bytes 131104 | tf_op jit(solution)/shard_map/ppermute | solution.py:450
  55.2 2.2 %collective-permute-done.6.refs_2_ = bf16[64,1024]{1,0:T(8,128)(2,1)S(1)} collective-permute-done((bf16[64,1024]{1,0:T(8,128)(2,1)S(1)}, bf16[64,1024]{1,0:T(8,128)(2,1)S(1)}, u32[]{:S(2)}, u32[]{:S(2)}) %collective-permute-start.6) | collective-permute-done | bytes 131104 | tf_op jit(solution)/shard_map/ppermute | solution.py:450
  57.4 0.1 collective-permute-done.7.refs_3_
  57.6 0.0 copy-start.12
  57.6 1.7 %layer_norm.1 = (bf16[64,1024]{1,0:T(8,128)(2,1)S(1)}, bf16[64,1024]{1,0:T(8,128)(2,1)S(1)}, bf16[8,128,768]{2,1,0:T(8,128)(2,1)S(1)}) custom-call(s32[8]{0:T(128)S(1)} %copy-done.9, s32[8]{0:T(128)S(1)} %copy-done.10, s32[8]{0:T(128)S(1)} %copy-done.11, bf16[64,64]{1,0:T(8,128)(2,1)S(1)} %copy-done.7, s32[64,1]{1,0:T(8,128)S(1)} %copy-done.5, ...), custom_call_target="tpu_custom_call" | custom-call | flops 100000000 | bytes 1000000 | tf_op jit(solution)/shard_map/layer_norm/pallas_call | solution.py:549
  59.3 1.7 %collective-permute-start.11 = (bf16[64,1024]{1,0:T(8,128)(2,1)S(1)}, bf16[64,1024]{1,0:T(8,128)(2,1)S(1)}, u32[]{:S(2)}, u32[]{:S(2)}) collective-permute-start(bf16[64,1024]{1,0:T(8,128)(2,1)S(1)} %get-tuple-element.59.refs_0_), channel_id=1, source_target_pairs={{0,24},{4,28},{8,0},{12,4},{16,8},{20,12},{24,16},{28,20},{1,25},{... | collective-permute-start | bytes 393224 | tf_op jit(solution)/shard_map/ppermute | solution.py:450
  61.0 1.5 %collective-permute-start.10 = (bf16[64,1024]{1,0:T(8,128)(2,1)S(1)}, bf16[64,1024]{1,0:T(8,128)(2,1)S(1)}, u32[]{:S(2)}, u32[]{:S(2)}) collective-permute-start(bf16[64,1024]{1,0:T(8,128)(2,1)S(1)} %get-tuple-element.59.refs_0_), channel_id=1, source_target_pairs={{0,16},{4,20},{8,24},{12,28},{16,0},{20,4},{24,8},{28,12},{1,17},{... | collective-permute-start | bytes 393224 | tf_op jit(solution)/shard_map/ppermute | solution.py:450
  62.5 0.7 collective-permute-start.12
  63.1 2.0 %collective-permute-done.11.refs_3_ = bf16[64,1024]{1,0:T(8,128)(2,1)S(1)} collective-permute-done((bf16[64,1024]{1,0:T(8,128)(2,1)S(1)}, bf16[64,1024]{1,0:T(8,128)(2,1)S(1)}, u32[]{:S(2)}, u32[]{:S(2)}) %collective-permute-start.11) | collective-permute-done | bytes 131104 | tf_op jit(solution)/shard_map/ppermute | solution.py:450
  65.1 4.4 %collective-permute-done.10.refs_2_ = bf16[64,1024]{1,0:T(8,128)(2,1)S(1)} collective-permute-done((bf16[64,1024]{1,0:T(8,128)(2,1)S(1)}, bf16[64,1024]{1,0:T(8,128)(2,1)S(1)}, u32[]{:S(2)}, u32[]{:S(2)}) %collective-permute-start.10) | collective-permute-done | bytes 131104 | tf_op jit(solution)/shard_map/ppermute | solution.py:450
  69.5 0.0 collective-permute-done.9.refs_1_
  69.5 2.0 %attention.1 = (bf16[64,256]{1,0:T(8,128)(2,1)S(1)}, bf16[64,256]{1,0:T(8,128)(2,1)S(1)}, bf16[64,256]{1,0:T(8,128)(2,1)S(1)}, bf16[64,256]{1,0:T(8,128)(2,1)S(1)}, bf16[8,1024,128]{2,1,0:T(8,128)(2,1)S(1)}) custom-call(s32[8]{0:T(128)S(1)} %copy-done.9, s32[8]{0:T(128)S(1)} %copy-done.10, s32[8]{0:T(128)S(1)} %copy-done.11, s32[1,64]{1,0:T(1,128)S(1)} %copy-done.12, ...), custom_call_target="tpu_custom_call" | custom-call | flops 1000000000 | bytes 2000000 | tf_op jit(solution)/shard_map/attention/pallas_call | solution.py:566
  71.5 0.7 collective-permute-start.13
  72.2 6.1 %collective-permute-start.14 = (bf16[64,256]{1,0:T(8,128)(2,1)S(1)}, bf16[64,256]{1,0:T(8,128)(2,1)S(1)}, u32[]{:S(2)}, u32[]{:S(2)}) collective-permute-start(bf16[64,256]{1,0:T(8,128)(2,1)S(1)} %get-tuple-element.63), channel_id=1, source_target_pairs={{0,3},{1,11},{2,19},{3,27},{4,7},{5,15},{6,23},{7,31},{8,0},{9,8},... | collective-permute-start | bytes 98312 | tf_op jit(solution)/shard_map/ppermute | solution.py:462
  78.3 1.7 %collective-permute-start.15 = (bf16[64,256]{1,0:T(8,128)(2,1)S(1)}, bf16[64,256]{1,0:T(8,128)(2,1)S(1)}, u32[]{:S(2)}, u32[]{:S(2)}) collective-permute-start(bf16[64,256]{1,0:T(8,128)(2,1)S(1)} %get-tuple-element.64), channel_id=1, source_target_pairs={{0,2},{1,10},{2,18},{3,26},{4,6},{5,14},{6,22},{7,30},{8,3},{9,11}... | collective-permute-start | bytes 98312 | tf_op jit(solution)/shard_map/ppermute | solution.py:462
  80.0 3.4 %collective-permute-start.16 = (bf16[64,256]{1,0:T(8,128)(2,1)S(1)}, bf16[64,256]{1,0:T(8,128)(2,1)S(1)}, u32[]{:S(2)}, u32[]{:S(2)}) collective-permute-start(bf16[64,256]{1,0:T(8,128)(2,1)S(1)} %get-tuple-element.65), channel_id=1, source_target_pairs={{0,1},{1,9},{2,17},{3,25},{4,5},{5,13},{6,21},{7,29},{8,2},{9,10},... | collective-permute-start | bytes 98312 | tf_op jit(solution)/shard_map/ppermute | solution.py:462
  83.4 0.0 collective-permute-done.12.rows_ref
  83.4 0.0 collective-permute-done.13.refs_0_
  83.4 1.6 %collective-permute-done.16.refs_3_ = bf16[64,256]{1,0:T(8,128)(2,1)S(1)} collective-permute-done((bf16[64,256]{1,0:T(8,128)(2,1)S(1)}, bf16[64,256]{1,0:T(8,128)(2,1)S(1)}, u32[]{:S(2)}, u32[]{:S(2)}) %collective-permute-start.16) | collective-permute-done | bytes 32800 | tf_op jit(solution)/shard_map/ppermute | solution.py:462
  85.0 1.9 %output.1 = (bf16[64,1024]{1,0:T(8,128)(2,1)}, bf16[64,1024]{1,0:T(8,128)(2,1)}) custom-call(s32[8]{0:T(128)S(1)} %copy-done.9, s32[8]{0:T(128)S(1)} %copy-done.10, s32[8]{0:T(128)S(1)} %copy-done.11, bf16[64,64]{1,0:T(8,128)(2,1)S(1)} %copy-done.7, s32[64,1]{1,0:T(8,128)S(1)} %copy-done.5, bf16[8,1024,128]{2,1,0:T(8,128)(2,1)S(1)} %get-tuple-element.60.weights_ref, ...), custom_call_target="tpu_custom_call" | custom-call | flops 100000000 | bytes 3000000 | tf_op jit(solution)/shard_map/output/pallas_call | solution.py:578
  (28 shorter events, 0.1 us)
Async XLA Ops:
  0.6 14.1 %copy-start.9 = (s32[8]{0:T(128)S(1)}, s32[8]{0:T(128)}, u32[]{:S(2)}) copy-start(s32[8]{0:T(128)} %slots_ref.7) | copy-start | bytes 100
  0.6 41.2 %collective-permute-start.1 = (bf16[640,1024]{1,0:T(8,128)(2,1)}, bf16[640,1024]{1,0:T(8,128)(2,1)S(1)}, u32[]{:S(2)}, u32[]{:S(2)}) collective-permute-start(bf16[640,1024]{1,0:T(8,128)(2,1)} %refs_0_.5), channel_id=1, source_target_pairs={{0,4},{4,0},{8,12},{12,8},{16,20},{20,16},{24,28},{28,24},{1,5},{5... | collective-permute-start | bytes 3932168 | tf_op jit(solution)/shard_map/ppermute | solution.py:454
  1.9 12.9 %collective-permute-start = (f32[8,384]{1,0:T(8,128)S(1)}, f32[8,384]{1,0:T(8,128)S(1)}, u32[]{:S(2)}, u32[]{:S(2)}) collective-permute-start(f32[8,384]{1,0:T(8,128)S(1)} %slice.3), channel_id=1, source_target_pairs={{0,1},{1,2},{2,3},{3,4},{4,5},{5,6},{6,7},{7,8},{8,9},{9,10},{10,1... | collective-permute-start | bytes 36872 | tf_op jit(solution)/shard_map/ppermute | solution.py:446
  6.4 1.2 %copy-start = (f32[512,512]{1,0:T(8,128)S(1)}, f32[512,512]{1,0:T(8,128)}, u32[]{:S(2)}) copy-start(f32[512,512]{1,0:T(8,128)} %constant.16.clone.refs_1_) | copy-start | bytes 3145732
  7.6 1.1 %copy-start.1 = (bf16[128,3072]{1,0:T(8,128)(2,1)S(1)}, bf16[128,3072]{1,0:T(8,128)(2,1)}, u32[]{:S(2)}) copy-start(bf16[128,3072]{1,0:T(8,128)(2,1)} %qkv_ref.1) | copy-start | bytes 2359300
  8.7 1.0 %copy-start.2 = (bf16[512,512]{1,0:T(8,128)(2,1)S(1)}, bf16[512,512]{1,0:T(8,128)(2,1)}, u32[]{:S(2)}) copy-start(bf16[512,512]{1,0:T(8,128)(2,1)} %constant.18.clone.refs_3_) | copy-start | bytes 1572868
  9.8 0.9 %copy-start.3 = (bf16[1024,128]{1,0:T(8,128)(2,1)S(1)}, bf16[1024,128]{1,0:T(8,128)(2,1)}, u32[]{:S(2)}) copy-start(bf16[1024,128]{1,0:T(8,128)(2,1)} %out_ref.1) | copy-start | bytes 786436
  10.7 0.9 %copy-start.4 = (f32[8,5120]{1,0:T(8,128)S(1)}, f32[8,5120]{1,0:T(8,128)}, u32[]{:S(2)}) copy-start(f32[8,5120]{1,0:T(8,128)} %refs_0_.3) | copy-start | bytes 491524
  11.6 0.9 %copy-start.6 = (f32[256,128]{1,0:T(8,128)S(1)}, f32[256,128]{1,0:T(8,128)}, u32[]{:S(2)}) copy-start(f32[256,128]{1,0:T(8,128)} %constant.17.clone.refs_2_) | copy-start | bytes 393220
  12.5 0.7 copy-start.8
  13.2 1.5 %copy-start.14 = (bf16[2304,256]{1,0:T(8,128)(2,1)S(1)}, bf16[2304,256]{1,0:T(8,128)(2,1)}, u32[]{:S(2)}) copy-start(bf16[2304,256]{1,0:T(8,128)(2,1)} %refs_0_.4) | copy-start | bytes 3538948
  13.2 1.5 %copy-start.15 = (bf16[288,512]{1,0:T(8,128)(2,1)S(1)}, bf16[288,512]{1,0:T(8,128)(2,1)}, u32[]{:S(2)}) copy-start(bf16[288,512]{1,0:T(8,128)(2,1)} %constant.19.clone.refs_1_) | copy-start | bytes 884740
  13.2 1.5 %copy-start.16 = (bf16[128,256]{1,0:T(8,128)(2,1)S(1)}, bf16[128,256]{1,0:T(8,128)(2,1)}, u32[]{:S(2)}) copy-start(bf16[128,256]{1,0:T(8,128)(2,1)} %constant.20.clone.refs_2_) | copy-start | bytes 196612
  14.8 27.1 %copy-start.13 = (bf16[640,1024]{1,0:T(8,128)(2,1)S(1)}, bf16[640,1024]{1,0:T(8,128)(2,1)}, u32[]{:S(2)}) copy-start(bf16[640,1024]{1,0:T(8,128)(2,1)} %refs_0_.5) | copy-start | bytes 3932164
  17.7 24.2 %collective-permute-start.2 = (bf16[1792,128]{1,0:T(8,128)(2,1)S(1)}, bf16[1792,128]{1,0:T(8,128)(2,1)S(1)}, u32[]{:S(2)}, u32[]{:S(2)}) collective-permute-start(bf16[1792,128]{1,0:T(8,128)(2,1)S(1)} %get-tuple-element.50), channel_id=1, source_target_pairs={{0,8},{4,12},{8,16},{12,20},{16,24},{20,28},{24,0},{28,4},{1,9},{5... | collective-permute-start | bytes 1376264 | tf_op jit(solution)/shard_map/ppermute | solution.py:450
  19.2 22.6 %collective-permute-start.3 = (bf16[1792,128]{1,0:T(8,128)(2,1)S(1)}, bf16[1792,128]{1,0:T(8,128)(2,1)S(1)}, u32[]{:S(2)}, u32[]{:S(2)}) collective-permute-start(bf16[1792,128]{1,0:T(8,128)(2,1)S(1)} %get-tuple-element.51), channel_id=1, source_target_pairs={{0,16},{4,20},{8,24},{12,28},{16,0},{20,4},{24,8},{28,12},{1,17},{... | collective-permute-start | bytes 1376264 | tf_op jit(solution)/shard_map/ppermute | solution.py:450
  20.8 21.1 %collective-permute-start.4 = (bf16[1792,128]{1,0:T(8,128)(2,1)S(1)}, bf16[1792,128]{1,0:T(8,128)(2,1)S(1)}, u32[]{:S(2)}, u32[]{:S(2)}) collective-permute-start(bf16[1792,128]{1,0:T(8,128)(2,1)S(1)} %get-tuple-element.52), channel_id=1, source_target_pairs={{0,24},{4,28},{8,0},{12,4},{16,8},{20,12},{24,16},{28,20},{1,25},{... | collective-permute-start | bytes 1376264 | tf_op jit(solution)/shard_map/ppermute | solution.py:450
  41.9 15.6 %copy-start.5 = (s32[64,1]{1,0:T(8,128)S(1)}, s32[64,1]{1,0:T(8,128)}, u32[]{:S(2)}) copy-start(s32[64,1]{1,0:T(8,128)} %constant.21.clone.sample_ref) | copy-start | bytes 772
  41.9 15.6 %copy-start.7 = (bf16[64,64]{1,0:T(8,128)(2,1)S(1)}, bf16[64,64]{1,0:T(8,128)(2,1)}, u32[]{:S(2)}) copy-start(bf16[64,64]{1,0:T(8,128)(2,1)} %constant.23.clone.frames_ref) | copy-start | bytes 24580
  41.9 15.6 %copy-start.10 = (s32[8]{0:T(128)S(1)}, s32[8]{0:T(128)}, u32[]{:S(2)}) copy-start(s32[8]{0:T(128)} %starts_ref.5) | copy-start | bytes 100
  41.9 15.6 %copy-start.11 = (s32[8]{0:T(128)S(1)}, s32[8]{0:T(128)}, u32[]{:S(2)}) copy-start(s32[8]{0:T(128)} %lengths_ref.5) | copy-start | bytes 100
  47.7 9.8 %collective-permute-start.8 = (bf16[4,1792,128]{2,1,0:T(8,128)(2,1)S(1)}, bf16[4,1792,128]{2,1,0:T(8,128)(2,1)S(1)}, u32[]{:S(2)}, u32[]{:S(2)}) collective-permute-start(bf16[4,1792,128]{2,1,0:T(8,128)(2,1)S(1)} %get-tuple-element.57.refs_4_), channel_id=1, source_target_pairs={{0,4},{4,0},{8,12},{12,8},{16,20},{20,16},{24,28},{28,24},{1,5},{5... | collective-permute-start | bytes 5505032 | tf_op jit(solution)/shard_map/ppermute | solution.py:454
  47.9 7.3 %collective-permute-start.5 = (bf16[64,1024]{1,0:T(8,128)(2,1)S(1)}, bf16[64,1024]{1,0:T(8,128)(2,1)S(1)}, u32[]{:S(2)}, u32[]{:S(2)}) collective-permute-start(bf16[64,1024]{1,0:T(8,128)(2,1)S(1)} %get-tuple-element.54), channel_id=1, source_target_pairs={{0,8},{4,12},{8,16},{12,20},{16,24},{20,28},{24,0},{28,4},{1,9},{5... | collective-permute-start | bytes 393224 | tf_op jit(solution)/shard_map/ppermute | solution.py:450
  49.6 7.8 %collective-permute-start.6 = (bf16[64,1024]{1,0:T(8,128)(2,1)S(1)}, bf16[64,1024]{1,0:T(8,128)(2,1)S(1)}, u32[]{:S(2)}, u32[]{:S(2)}) collective-permute-start(bf16[64,1024]{1,0:T(8,128)(2,1)S(1)} %get-tuple-element.55), channel_id=1, source_target_pairs={{0,16},{4,20},{8,24},{12,28},{16,0},{20,4},{24,8},{28,12},{1,17},{... | collective-permute-start | bytes 393224 | tf_op jit(solution)/shard_map/ppermute | solution.py:450
  50.2 7.4 %collective-permute-start.7 = (bf16[64,1024]{1,0:T(8,128)(2,1)S(1)}, bf16[64,1024]{1,0:T(8,128)(2,1)S(1)}, u32[]{:S(2)}, u32[]{:S(2)}) collective-permute-start(bf16[64,1024]{1,0:T(8,128)(2,1)S(1)} %get-tuple-element.56), channel_id=1, source_target_pairs={{0,24},{4,28},{8,0},{12,4},{16,8},{20,12},{24,16},{28,20},{1,25},{... | collective-permute-start | bytes 393224 | tf_op jit(solution)/shard_map/ppermute | solution.py:450
  57.6 12.0 %copy-start.12 = (s32[1,64]{1,0:T(1,128)S(1)}, s32[1,64]{1,0:T(1,128)}, u32[]{:S(2)}) copy-start(s32[1,64]{1,0:T(1,128)} %constant.22.clone.sample_ref) | copy-start | bytes 772
  59.3 5.9 %collective-permute-start.11 = (bf16[64,1024]{1,0:T(8,128)(2,1)S(1)}, bf16[64,1024]{1,0:T(8,128)(2,1)S(1)}, u32[]{:S(2)}, u32[]{:S(2)}) collective-permute-start(bf16[64,1024]{1,0:T(8,128)(2,1)S(1)} %get-tuple-element.59.refs_0_), channel_id=1, source_target_pairs={{0,24},{4,28},{8,0},{12,4},{16,8},{20,12},{24,16},{28,20},{1,25},{... | collective-permute-start | bytes 393224 | tf_op jit(solution)/shard_map/ppermute | solution.py:450
  61.0 8.6 %collective-permute-start.10 = (bf16[64,1024]{1,0:T(8,128)(2,1)S(1)}, bf16[64,1024]{1,0:T(8,128)(2,1)S(1)}, u32[]{:S(2)}, u32[]{:S(2)}) collective-permute-start(bf16[64,1024]{1,0:T(8,128)(2,1)S(1)} %get-tuple-element.59.refs_0_), channel_id=1, source_target_pairs={{0,16},{4,20},{8,24},{12,28},{16,0},{20,4},{24,8},{28,12},{1,17},{... | collective-permute-start | bytes 393224 | tf_op jit(solution)/shard_map/ppermute | solution.py:450
  62.5 7.1 %collective-permute-start.9 = (bf16[64,1024]{1,0:T(8,128)(2,1)S(1)}, bf16[64,1024]{1,0:T(8,128)(2,1)S(1)}, u32[]{:S(2)}, u32[]{:S(2)}) collective-permute-start(bf16[64,1024]{1,0:T(8,128)(2,1)S(1)} %get-tuple-element.59.refs_0_), channel_id=1, source_target_pairs={{0,8},{4,12},{8,16},{12,20},{16,24},{20,28},{24,0},{28,4},{1,9},{5... | collective-permute-start | bytes 393224 | tf_op jit(solution)/shard_map/ppermute | solution.py:450
  62.5 20.9 %collective-permute-start.12 = (bf16[64,1024]{1,0:T(8,128)(2,1)S(1)}, bf16[64,1024]{1,0:T(8,128)(2,1)S(1)}, u32[]{:S(2)}, u32[]{:S(2)}) collective-permute-start(bf16[64,1024]{1,0:T(8,128)(2,1)S(1)} %get-tuple-element.61), channel_id=1, source_target_pairs={{0,0},{1,8},{2,16},{3,24},{4,4},{5,12},{6,20},{7,28},{8,1},{9,9},{... | collective-permute-start | bytes 393224 | tf_op jit(solution)/shard_map/ppermute | solution.py:462
  71.5 11.9 %collective-permute-start.13 = (bf16[64,256]{1,0:T(8,128)(2,1)S(1)}, bf16[64,256]{1,0:T(8,128)(2,1)S(1)}, u32[]{:S(2)}, u32[]{:S(2)}) collective-permute-start(bf16[64,256]{1,0:T(8,128)(2,1)S(1)} %get-tuple-element.62), channel_id=1, source_target_pairs={{0,0},{1,8},{2,16},{3,24},{4,4},{5,12},{6,20},{7,28},{8,1},{9,9},{... | collective-permute-start | bytes 98312 | tf_op jit(solution)/shard_map/ppermute | solution.py:462
  72.2 11.2 %collective-permute-start.14 = (bf16[64,256]{1,0:T(8,128)(2,1)S(1)}, bf16[64,256]{1,0:T(8,128)(2,1)S(1)}, u32[]{:S(2)}, u32[]{:S(2)}) collective-permute-start(bf16[64,256]{1,0:T(8,128)(2,1)S(1)} %get-tuple-element.63), channel_id=1, source_target_pairs={{0,3},{1,11},{2,19},{3,27},{4,7},{5,15},{6,23},{7,31},{8,0},{9,8},... | collective-permute-start | bytes 98312 | tf_op jit(solution)/shard_map/ppermute | solution.py:462
  78.3 5.1 %collective-permute-start.15 = (bf16[64,256]{1,0:T(8,128)(2,1)S(1)}, bf16[64,256]{1,0:T(8,128)(2,1)S(1)}, u32[]{:S(2)}, u32[]{:S(2)}) collective-permute-start(bf16[64,256]{1,0:T(8,128)(2,1)S(1)} %get-tuple-element.64), channel_id=1, source_target_pairs={{0,2},{1,10},{2,18},{3,26},{4,6},{5,14},{6,22},{7,30},{8,3},{9,11}... | collective-permute-start | bytes 98312 | tf_op jit(solution)/shard_map/ppermute | solution.py:462
  80.0 5.0 %collective-permute-start.16 = (bf16[64,256]{1,0:T(8,128)(2,1)S(1)}, bf16[64,256]{1,0:T(8,128)(2,1)S(1)}, u32[]{:S(2)}, u32[]{:S(2)}) collective-permute-start(bf16[64,256]{1,0:T(8,128)(2,1)S(1)} %get-tuple-element.65), channel_id=1, source_target_pairs={{0,1},{1,9},{2,17},{3,25},{4,5},{5,13},{6,21},{7,29},{8,2},{9,10},... | collective-permute-start | bytes 98312 | tf_op jit(solution)/shard_map/ppermute | solution.py:462
where the time goes:
time: 87.4 us; the launch traced here: 86.9 us
  starting transfers between devices  29.8 us (34%)
  blocking collectives  19.7 us (23%)
  Pallas kernels  15.7 us (18%)
  waiting for transfers between devices  13.2 us (15%)
  local copies, waits for them, and re-layouts  7.62 us (9%)
    all_to_all x1, blocking collectives, on_device(): lax.all_to_all(mel, ('dp', 'seq'), split_axis=0, concat_axis=0, tiled=True)  19.7 us
    ppermute x5, starting transfers between devices, to_owner(): return lax.ppermute(block, ('dp', 'seq'), pairs)  12.5 us
    ppermute x9, starting transfers between devices, to_part(): return lax.ppermute(block, 'dp', pairs)  12.1 us
    ppermute x9, waiting for transfers between devices, to_part(): return lax.ppermute(block, 'dp', pairs)  11.6 us
    unnamed x34, local copies, waits for them, and re-layouts  6.91 us
    pallas_call x1, Pallas kernels, on_device(): pl.pallas_call(functools.partial(conv_kernel, parts, width, windows), out...  5.78 us
    ppermute x1, starting transfers between devices, on_device(): rim = lax.ppermute(audio[:, audio.shape[1] - RIM:], ('dp', 'seq'), route)  4.48 us
    pallas_call x1, Pallas kernels, on_device(): pl.pallas_call(functools.partial(mel_kernel, parts, group, len(later_tabl...  2.91 us
  transfers between devices with their start and end apart: 17, of which 6 were waited for; matrix products, arithmetic and copies ran while one was open for 1% of the time, Pallas kernels for 7%

commit v1 on v0

--- a/solution.py
+++ b/solution.py
@@ -160,49 +160,45 @@
     ]
 
 
-def prep_kernel(parts, width, tables, conv1_ref, qkv_ref, out_ref, *refs):
-    table_refs, refs = refs[:tables], refs[tables:]
-    table_outs, refs = refs[:tables], refs[tables:]
-    pack_outs, (banded_out, sems) = refs[:parts], refs[parts:]
+def prep_kernel(parts, qkv_ref, *refs):
+    mix_outs, sems = refs[:parts], refs[parts]
     part, _ = place(parts)
-    rows = qkv_ref.shape[0]
     features = qkv_ref.shape[1] // 3
     head_width = features // parts
-    blocks = head_width // LANES
-    copies = loads_of(table_refs, table_outs, sems, 0)
+    copies = []
     for step in range(parts):
         first = pl.multiple_of(later(part, step, parts) * head_width, LANES)
         for kind in range(3):
-            for piece in range(blocks):
-                source = qkv_ref.at[:, pl.ds(kind * features + first + piece * LANES, LANES)]
-                target = pack_outs[step].at[pl.ds((kind * blocks + piece) * rows, rows)]
-                copies.append(pltpu.make_async_copy(source, target, sems.at[len(copies)]))
-        target = pack_outs[step].at[pl.ds(3 * blocks * rows, out_ref.shape[0])]
-        copies.append(pltpu.make_async_copy(out_ref, target, sems.at[len(copies)]))
+            source = qkv_ref.at[:, pl.ds(kind * features + first, head_width)]
+            target = mix_outs[step].at[:, pl.ds(kind * head_width, head_width)]
+            copies.append(pltpu.make_async_copy(source, target, sems.at[len(copies)]))
     start_all(copies)
+    wait_all(copies)
+
+
+def banded_weights(width, conv1_ref, banded_out):
     taps, channels = conv1_ref.shape
-    outs = banded_out.shape[1] // channels
     row = lax.broadcasted_iota(jnp.int32, (LANES, taps), 0)
     tap = lax.broadcasted_iota(jnp.int32, (LANES, taps), 1)
     line = (tap >= 3).astype(jnp.int32) + (tap >= 6).astype(jnp.int32)
     target = line * (width - 3) + tap + 1
     weight = conv1_ref[...]
-    for g in range(outs):
+    for g in range(banded_out.shape[1] // channels):
         select = (row == target + 2 * g).astype(F32).astype(BF16)
         banded_out[:, g * channels : (g + 1) * channels] = jnp.dot(
             select, weight, preferred_element_type=F32
         ).astype(BF16)
-    wait_all(copies)
 
 
 def mel_kernel(
-    parts, group, tables, slots_ref, rim_ref, audio_ref, table_ref, filter_ref, select_ref, *refs
+    parts, group, width, tables, slots_ref, rim_ref, audio_ref, table_ref, filter_ref, select_ref, conv1_ref, *refs
 ):
     table_refs, refs = refs[:tables], refs[tables:]
-    out_ref, refs = refs[0], refs[1:]
+    (out_ref, banded_out), refs = refs[:2], refs[2:]
     table_outs, (ext, sems) = refs[:tables], refs[tables:]
     loads = loads_of(table_refs, table_outs, sems, 0)
     start_all(loads)
+    banded_weights(width, conv1_ref, banded_out)
     streams = audio_ref.shape[0]
     rows = W * streams
     ext[:, :RIM] = rim_ref[...]
@@ -247,20 +243,26 @@
     wait_all(loads)
 
 
+def stacked(parts, pieces, stack_out, sems, base):
+    part, _ = place(parts)
+    return [
+        pltpu.make_async_copy(pieces[step], stack_out.at[later(part, parts - step, parts)], sems.at[base + step])
+        for step in range(parts)
+    ]
+
+
 def conv_kernel(parts, width, windows, mel_ref, banded_ref, conv2, rows_ref, shift_ref, *refs):
     part, copy_index = place(parts)
     copies = lax.axis_size("dp") // parts
     proj_refs, refs = refs[:copies], refs[copies:]
-    pack_refs, refs = refs[:parts], refs[parts:]
+    weight_refs, refs = refs[:parts], refs[parts:]
     outs_refs, refs = refs[:parts], refs[parts:]
     stack_out, even, odd, second, proj, partial, sems = refs
     loads = []
     for step in range(copies):
         slot = later(copy_index, copies - step, copies)
         loads.append(pltpu.make_async_copy(proj_refs[step], proj.at[slot], sems.at[step]))
-    for step in range(parts):
-        slot = later(part, parts - step, parts)
-        loads.append(pltpu.make_async_copy(pack_refs[step], stack_out.at[slot], sems.at[copies + step]))
+    loads += stacked(parts, weight_refs, stack_out, sems, copies)
     start_all(loads)
     sources = mel_ref.shape[0]
     n = sources
@@ -310,30 +312,15 @@
     return begin, begin + span
 
 
-def place_mix(parts, rows, stack_refs, buffer, sems, base):
+def placed(parts, stack_refs, buffer, sems, base):
     _, copy_index = place(parts)
     copies = len(stack_refs)
     moves = []
     for step in range(copies):
         slot = later(copy_index, copies - step, copies)
         for piece in range(parts):
-            for block in range(buffer.shape[2] // LANES):
-                source = stack_refs[step].at[piece, pl.ds(block * rows, rows)]
-                target = buffer.at[piece * copies + slot, :, pl.ds(block * LANES, LANES)]
-                moves.append(pltpu.make_async_copy(source, target, sems.at[base + len(moves)]))
-    return moves
-
-
-def place_out(parts, rows, stack_refs, buffer, sems, base):
-    _, copy_index = place(parts)
-    copies = len(stack_refs)
-    moves = []
-    for step in range(copies):
-        slot = later(copy_index, copies - step, copies)
-        for piece in range(parts):
-            source = stack_refs[step].at[piece, pl.ds(rows, buffer.shape[1])]
             target = buffer.at[piece * copies + slot]
-            moves.append(pltpu.make_async_copy(source, target, sems.at[base + len(moves)]))
+            moves.append(pltpu.make_async_copy(stack_refs[step].at[piece], target, sems.at[base + len(moves)]))
     return moves
 
 
@@ -341,9 +328,9 @@
     part, copy_index = place(parts)
     copies = lax.axis_size("dp") // parts
     part_refs, refs = refs[:parts], refs[parts:]
-    stack_refs, refs = refs[:copies], refs[copies:]
-    rows_out, normed_out, mix_out, sems = refs
-    moves = place_mix(parts, mix_out.shape[1], stack_refs, mix_out, sems, 0)
+    piece_refs, refs = refs[:parts], refs[parts:]
+    rows_out, normed_out, stack_out, sems = refs
+    moves = stacked(parts, piece_refs, stack_out, sems, 0)
     start_all(moves)
     row = lax.axis_index("seq") * copies + copy_index
     begin, end = bounds(row, slots_ref, starts_ref, lengths_ref)
@@ -363,13 +350,16 @@
     wait_all(moves)
 
 
-def attention_kernel(parts, mix_rows, slots_ref, starts_ref, lengths_ref, sample_ref, mix_ref, *refs):
+def attention_kernel(parts, slots_ref, starts_ref, lengths_ref, sample_ref, *refs):
     part, copy_index = place(parts)
     copies = lax.axis_size("dp") // parts
     normed_refs, refs = refs[:parts], refs[parts:]
+    mix_refs, refs = refs[:copies], refs[copies:]
     stack_refs, refs = refs[:copies], refs[copies:]
-    outs_refs, (weights_out, sems) = refs[:parts], refs[parts:]
-    moves = place_out(parts, mix_rows, stack_refs, weights_out, sems, 0)
+    outs_refs, (weights_out, mix, sems) = refs[:parts], refs[parts:]
+    loads = placed(parts, mix_refs, mix, sems, 0)
+    start_all(loads)
+    moves = placed(parts, stack_refs, weights_out, sems, len(loads))
     start_all(moves)
     row = lax.axis_index("seq") * copies + copy_index
     begin, end = bounds(row, slots_ref, starts_ref, lengths_ref)
@@ -381,9 +371,10 @@
     valid = jnp.concatenate(masks, axis=1) > 0.5
     normed = jnp.concatenate([ref[...] for ref in normed_refs], axis=0)
     local, features = normed_refs[0].shape
-    weights = mix_ref[...].reshape(features, mix_ref.shape[2])
+    wait_all(loads)
+    weights = mix[...].reshape(features, mix.shape[2])
     mixed = jnp.dot(normed, weights, preferred_element_type=F32).astype(BF16)
-    width = mix_ref.shape[2] // 3
+    width = mix.shape[2] // 3
     scale = HEAD_DIM ** (-0.5)
     for head in range(width // HEAD_DIM):
         at = head * HEAD_DIM
@@ -467,62 +458,58 @@
     def like(array):
         return jax.ShapeDtypeStruct(array.shape, array.dtype)
 
+    mix_piece = jax.ShapeDtypeStruct((qkv_weight.shape[0], 3 * head_width), BF16)
+    mix_parts = pl.pallas_call(
+        functools.partial(prep_kernel, parts),
+        out_shape=tuple([mix_piece] * parts),
+        in_specs=[anywhere()],
+        out_specs=tuple([anywhere()] * parts),
+        scratch_shapes=[pltpu.SemaphoreType.DMA((3 * parts,))],
+        compiler_params=params(4),
+        cost_estimate=cost(1e8, 2e7),
+        name="prep",
+    )(qkv_weight)
+    mix_parts, rim, out_here = lax.optimization_barrier((mix_parts, rim, out_weight))
+    out_all = [out_here] + [to_part(out_here, step) for step in range(1, parts)]
+    mix_all = [mix_parts[0]] + [to_part(mix_parts[step], step) for step in range(1, parts)]
+
     tables = [
+        conv2_weight,
+        jnp.asarray(row_selection(windows, group)),
+        jnp.asarray(shift_selection(width)),
+    ]
+    banded = jax.ShapeDtypeStruct((LANES, outs * channels), BF16)
+    mel, banded, *tables = pl.pallas_call(
+        functools.partial(mel_kernel, parts, group, width, len(tables)),
+        out_shape=tuple(
+            [jax.ShapeDtypeStruct((sources, W, LANES), BF16), banded] + [like(table) for table in tables]
+        ),
+        in_specs=[smem()] + [vmem()] * 6 + [hbm()] * len(tables),
+        out_specs=tuple([vmem()] * (2 + len(tables))),
+        scratch_shapes=[
+            pltpu.VMEM((streams, RIM + audio.shape[1]), F32),
+            pltpu.SemaphoreType.DMA((len(tables),)),
+        ],
+        compiler_params=params(min(20 * scale, 48)),
+        cost_estimate=cost(2e9, 2e6),
+        name="log_mel",
+    )(
+        slots,
+        rim,
         audio,
         jnp.asarray(spectrum_table(N_FFT)),
         jnp.asarray(filter_table()),
         jnp.asarray(band_selection(parts)),
-    ]
-    mix_rows = 3 * head_width // LANES * qkv_weight.shape[0]
-    out_packed = out_weight.reshape(-1, LANES)
-    pack = jax.ShapeDtypeStruct((mix_rows + out_packed.shape[0], LANES), BF16)
-    prepared = pl.pallas_call(
-        functools.partial(prep_kernel, parts, width, len(tables)),
-        out_shape=tuple(
-            [like(table) for table in tables]
-            + [pack] * parts
-            + [jax.ShapeDtypeStruct((LANES, outs * channels), BF16)]
-        ),
-        in_specs=[vmem()] + [hbm()] * (2 + len(tables)),
-        out_specs=tuple([vmem()] * len(tables) + [anywhere()] * parts + [vmem()]),
-        scratch_shapes=[
-            pltpu.SemaphoreType.DMA((len(tables) + parts * (3 * head_width // LANES + 1),))
-        ],
-        compiler_params=params(min(16 * scale, 32)),
-        cost_estimate=cost(1e8, 4e6),
-        name="prep",
-    )(conv1_weight, qkv_weight, out_packed, *tables)
-    tables, packs, banded = prepared[: len(tables)], prepared[len(tables) : -1], prepared[-1]
-
-    later_tables = [
-        conv2_weight,
-        jnp.asarray(row_selection(windows, group)),
-        jnp.asarray(shift_selection(width)),
-    ]
-    mel, *later_tables = pl.pallas_call(
-        functools.partial(mel_kernel, parts, group, len(later_tables)),
-        out_shape=tuple(
-            [jax.ShapeDtypeStruct((sources, W, LANES), BF16)] + [like(table) for table in later_tables]
-        ),
-        in_specs=[smem()] + [vmem()] * (1 + len(tables)) + [hbm()] * len(later_tables),
-        out_specs=tuple([vmem()] * (1 + len(later_tables))),
-        scratch_shapes=[
-            pltpu.VMEM((streams, RIM + audio.shape[1]), F32),
-            pltpu.SemaphoreType.DMA((len(later_tables),)),
-        ],
-        compiler_params=params(min(20 * scale, 48)),
-        cost_estimate=cost(2e9, 2e6),
-        name="log_mel",
-    )(slots, rim, *tables, *later_tables)
-    mel, *packs = lax.optimization_barrier((mel, *packs))
+        conv1_weight,
+        *tables,
+    )
     mel = lax.all_to_all(mel, ("dp", "seq"), split_axis=0, concat_axis=0, tiled=True)
-    packs = [packs[0]] + [to_part(packs[step], step) for step in range(1, parts)]
 
     block = jax.ShapeDtypeStruct((local, features), BF16)
     *partials, stack = pl.pallas_call(
         functools.partial(conv_kernel, parts, width, windows),
-        out_shape=tuple([block] * parts + [jax.ShapeDtypeStruct((parts,) + pack.shape, BF16)]),
-        in_specs=[vmem()] * (2 + len(later_tables)) + [anywhere()] * (copies + parts),
+        out_shape=tuple([block] * parts + [jax.ShapeDtypeStruct((parts,) + out_weight.shape, BF16)]),
+        in_specs=[vmem()] * (2 + len(tables)) + [anywhere()] * (copies + parts),
         out_specs=tuple([vmem()] * parts + [anywhere()]),
         scratch_shapes=[
             pltpu.VMEM((JS * n, banded.shape[1]), BF16),
@@ -535,8 +522,8 @@
         compiler_params=params(min(24 * scale, 48)),
         cost_estimate=cost(8e9, 4e6),
         name="conv",
-    )(mel, banded, *later_tables, *proj_all, *packs)
-    stacks = [stack] + [to_copy(stack, step) for step in range(1, copies)]
+    )(mel, banded, *tables, *proj_all, *out_all)
+    out_stacks = [stack] + [to_copy(stack, step) for step in range(1, copies)]
     partials = [partials[0]] + [to_part(partials[step], step) for step in range(1, parts)]
 
     index = np.arange(local)
@@ -545,34 +532,34 @@
     out_sample = jnp.asarray(out_sample.reshape(-1, 1).astype(np.int32))
     key_sample = jnp.asarray(key_sample.reshape(1, -1).astype(np.int32))
     frames = jnp.asarray(frame_table(windows))
-    mix = jax.ShapeDtypeStruct((windows, qkv_weight.shape[0], 3 * head_width), BF16)
-    regrouped, normed, mix = pl.pallas_call(
+    regrouped, normed, stack = pl.pallas_call(
         functools.partial(norm_kernel, parts),
-        out_shape=(block, block, mix),
-        in_specs=[smem()] * 3 + [vmem()] * (2 + parts) + [anywhere()] * copies,
-        out_specs=(vmem(), vmem(), vmem()),
-        scratch_shapes=[pltpu.SemaphoreType.DMA((windows * (3 * head_width // LANES),))],
+        out_shape=(block, block, jax.ShapeDtypeStruct((parts,) + mix_piece.shape, BF16)),
+        in_specs=[smem()] * 3 + [vmem()] * (2 + parts) + [anywhere()] * parts,
+        out_specs=(vmem(), vmem(), anywhere()),
+        scratch_shapes=[pltpu.SemaphoreType.DMA((parts,))],
         compiler_params=params(min(12 * scale, 32)),
         cost_estimate=cost(1e8, 1e6),
         name="layer_norm",
-    )(slots, starts, lengths, frames, out_sample, *partials, *stacks)
+    )(slots, starts, lengths, frames, out_sample, *partials, *mix_all)
+    mix_stacks = [stack] + [to_copy(stack, step) for step in range(1, copies)]
     normed = [normed] + [to_part(normed, step) for step in range(1, parts)]
     regrouped = to_owner(regrouped, 0)
 
     out_columns = jax.ShapeDtypeStruct((windows,) + out_weight.shape, BF16)
-    if out_packed.shape != out_weight.shape:
-        stacks = [stack[:, mix_rows:].reshape((parts,) + out_weight.shape) for stack in stacks]
-        mix_rows = 0
     *context, out_columns = pl.pallas_call(
-        functools.partial(attention_kernel, parts, mix_rows),
+        functools.partial(attention_kernel, parts),
         out_shape=tuple([jax.ShapeDtypeStruct((local, head_width), BF16)] * parts + [out_columns]),
-        in_specs=[smem()] * 3 + [vmem()] * (2 + parts) + [anywhere()] * copies,
+        in_specs=[smem()] * 3 + [vmem()] * (1 + parts) + [anywhere()] * (2 * copies),
         out_specs=tuple([vmem()] * (parts + 1)),
-        scratch_shapes=[pltpu.SemaphoreType.DMA((windows,))],
+        scratch_shapes=[
+            pltpu.VMEM((windows,) + mix_piece.shape, BF16),
+            pltpu.SemaphoreType.DMA((2 * windows,)),
+        ],
         compiler_params=params(min(16 * scale, 48)),
         cost_estimate=cost(1e9, 2e6),
         name="attention",
-    )(slots, starts, lengths, key_sample, mix, *normed, *stacks)
+    )(slots, starts, lengths, key_sample, *normed, *mix_stacks, *out_stacks)
     context = [to_owner(context[step], step) for step in range(parts)]
 
     regrouped, attended = pl.pallas_call(

time: 87.4 us -> 94.2 us (1.078)
  blocking collectives: 19.7 us -> 0 us
  local copies, waits for them, and re-layouts: 7.62 us -> 17.9 us
  waiting for transfers between devices: 13.2 us -> 21.7 us
  starting transfers between devices: 29.8 us -> 34.5 us
  Pallas kernels: 15.7 us -> 18.1 us
    all_to_all x1 -> x0, blocking collectives: 19.7 us -> none  [on_device(): lax.all_to_all(mel, ('dp', 'seq'), split_axis=0, concat_axis=0, tiled=True)]
    unnamed x34 -> x58, local copies, waits for them, and re-layouts: 6.91 us -> 17.2 us
    ppermute x9 -> x12, starting transfers between devices: 12.1 us -> 17.4 us  [to_part(): return lax.ppermute(block, 'dp', pairs)]
    all_to_all x0 -> x1, waiting for transfers between devices: none -> 4.26 us  [on_device(): lax.all_to_all(mel, ('dp', 'seq'), split_axis=0, concat_axis=0, tiled=True)]
    ppermute x5, starting transfers between devices: 12.5 us -> 9.16 us  [to_owner(): return lax.ppermute(block, ('dp', 'seq'), pairs)]
    all_to_all x0 -> x1, starting transfers between devices: none -> 2.77 us  [on_device(): lax.all_to_all(mel, ('dp', 'seq'), split_axis=0, concat_axis=0, tiled=True)]
    ppermute x9 -> x12, waiting for transfers between devices: 11.6 us -> 14.1 us  [to_part(): return lax.ppermute(block, 'dp', pairs)]
    pallas_call x3, Pallas kernels: 6.36 us -> 8.66 us  [the longest x1 4.19 us: on_device(): pl.pallas_call(functools.partial(attention_kernel, parts), out_shape=tupl...]
  transfers between devices with their start and end apart: 17 -> 22, of which waited for: 6 -> 8; matrix products, arithmetic and copies ran while one was open for 1% -> 1% of each run, Pallas kernels for 7% -> 17%
where the time goes in v1:
time: 94.2 us; the launch traced here: 93 us
  starting transfers between devices  34.5 us (37%)
  waiting for transfers between devices  21.7 us (23%)
  Pallas kernels  18.1 us (19%)
  local copies, waits for them, and re-layouts  17.9 us (19%)
    ppermute x12, starting transfers between devices, to_part(): return lax.ppermute(block, 'dp', pairs)  17.4 us
    unnamed x58, local copies, waits for them, and re-layouts  17.2 us
    ppermute x12, waiting for transfers between devices, to_part(): return lax.ppermute(block, 'dp', pairs)  14.1 us
    ppermute x5, starting transfers between devices, to_owner(): return lax.ppermute(block, ('dp', 'seq'), pairs)  9.16 us
    pallas_call x1, Pallas kernels, on_device(): pl.pallas_call(functools.partial(conv_kernel, parts, width, windows), out...  5.58 us
    ppermute x1, starting transfers between devices, on_device(): rim = lax.ppermute(audio[:, audio.shape[1] - RIM:], ('dp', 'seq'), route)  4.48 us
    all_to_all x1, waiting for transfers between devices, on_device(): lax.all_to_all(mel, ('dp', 'seq'), split_axis=0, concat_axis=0, tiled=True)  4.26 us
    pallas_call x1, Pallas kernels, on_device(): pl.pallas_call(functools.partial(attention_kernel, parts), out_shape=tupl...  4.19 us
  transfers between devices with their start and end apart: 22, of which 8 were waited for; matrix products, arithmetic and copies ran while one was open for 1% of the time, Pallas kernels for 17%

profile of v1, /device:TPU:0, one launch (start us, length us, event | category | flops | bytes accessed | tf_op | source)
XLA Modules:
  0.0 93.0 jit_solution(692114119259010757)
XLA Ops:
  1.1 0.7 slice.3
  1.9 4.5 %collective-permute-start = (f32[8,384]{1,0:T(8,128)S(1)}, f32[8,384]{1,0:T(8,128)S(1)}, u32[]{:S(2)}, u32[]{:S(2)}) collective-permute-start(f32[8,384]{1,0:T(8,128)S(1)} %slice.3), channel_id=1, source_target_pairs={{0,1},{1,2},{2,3},{3,4},{4,5},{5,6},{6,7},{7,8},{8,9},{9,10},{10,1... | collective-permute-start | bytes 36872 | tf_op jit(solution)/shard_map/ppermute | solution.py:437
  6.4 1.1 %copy-done = bf16[128,3072]{1,0:T(8,128)(2,1)S(1)} copy-done((bf16[128,3072]{1,0:T(8,128)(2,1)S(1)}, bf16[128,3072]{1,0:T(8,128)(2,1)}, u32[]{:S(2)}) %copy-start) | copy-done | bytes 786456
  7.5 0.8 prep.1
  8.3 0.7 copy-done.12
  9.0 4.0 %collective-permute-start.4 = (bf16[1024,128]{1,0:T(8,128)(2,1)}, bf16[1024,128]{1,0:T(8,128)(2,1)}, u32[]{:S(2)}, u32[]{:S(2)}) collective-permute-start(bf16[1024,128]{1,0:T(8,128)(2,1)} %refs_2_.1), channel_id=1, source_target_pairs={{0,24},{4,28},{8,0},{12,4},{16,8},{20,12},{24,16},{28,20},{1,25},{... | collective-permute-start | bytes 786440 | tf_op jit(solution)/shard_map/ppermute | solution.py:441
  13.5 1.5 %collective-permute-start.2 = (bf16[1024,128]{1,0:T(8,128)(2,1)}, bf16[1024,128]{1,0:T(8,128)(2,1)}, u32[]{:S(2)}, u32[]{:S(2)}) collective-permute-start(bf16[1024,128]{1,0:T(8,128)(2,1)} %refs_2_.1), channel_id=1, source_target_pairs={{0,8},{4,12},{8,16},{12,20},{16,24},{20,28},{24,0},{28,4},{1,9},{5... | collective-permute-start | bytes 786440 | tf_op jit(solution)/shard_map/ppermute | solution.py:441
  15.0 0.7 copy-done.3
  15.7 0.9 copy-done.7
  16.6 1.3 %copy-done.10 = bf16[2304,256]{1,0:T(8,128)(2,1)S(1)} copy-done((bf16[2304,256]{1,0:T(8,128)(2,1)S(1)}, bf16[2304,256]{1,0:T(8,128)(2,1)}, u32[]{:S(2)}) %copy-start.10) | copy-done | bytes 1179672
  17.9 0.7 copy-done.15
  18.6 1.2 %copy-done.16 = f32[512,512]{1,0:T(8,128)S(1)} copy-done((f32[512,512]{1,0:T(8,128)S(1)}, f32[512,512]{1,0:T(8,128)}, u32[]{:S(2)}) %copy-start.16) | copy-done | bytes 1048600
  19.8 1.0 %copy-done.17 = bf16[512,512]{1,0:T(8,128)(2,1)S(1)} copy-done((bf16[512,512]{1,0:T(8,128)(2,1)S(1)}, bf16[512,512]{1,0:T(8,128)(2,1)}, u32[]{:S(2)}) %copy-start.17) | copy-done | bytes 524312
  20.8 1.0 %copy-done.18 = bf16[288,512]{1,0:T(8,128)(2,1)S(1)} copy-done((bf16[288,512]{1,0:T(8,128)(2,1)S(1)}, bf16[288,512]{1,0:T(8,128)(2,1)}, u32[]{:S(2)}) %copy-start.18) | copy-done | bytes 294936
  21.8 0.9 copy-done.19
  22.7 0.8 copy-done.20
  23.5 3.6 %log_mel.1 = (bf16[32,8,128]{2,1,0:T(8,128)(2,1)}, bf16[128,2816]{1,0:T(8,128)(2,1)S(1)}, bf16[2304,256]{1,0:T(8,128)(2,1)S(1)}, bf16[288,512]{1,0:T(8,128)(2,1)S(1)}, bf16[128,256]{1,0:T(8,128)(2,1)S(1)}) custom-call(s32[8]{0:T(128)S(1)} %copy-done.3, f32[8,384]{1,0:T(8,128)S(1)} %collective-permute-done.rim_ref, f32[8,5120]{1,0:T(8,128)S(1)} %copy-done.7, ...), custom_call_target="tpu_custom_call" | custom-call | flops 2000000000 | bytes 2000000 | tf_op jit(solution)/shard_map/log_mel/pallas_call | solution.py:482
  27.2 1.1 %copy-done.21 = bf16[2304,256]{1,0:T(8,128)(2,1)} copy-done((bf16[2304,256]{1,0:T(8,128)(2,1)}, bf16[2304,256]{1,0:T(8,128)(2,1)S(1)}, u32[]{:S(2)}) %copy-start.21) | copy-done | bytes 1179672
  28.2 0.9 copy-done.23
  29.1 0.7 copy-done.25
  29.8 2.8 %all-to-all-start = ((bf16[32,8,128]{2,1,0:T(8,128)(2,1)}), bf16[32,8,128]{2,1,0:T(8,128)(2,1)S(1)}, u32[]{:S(2)}, u32[]{:S(2)}) async-start(bf16[32,8,128]{2,1,0:T(8,128)(2,1)} %get-tuple-element.37), calls=%async_computation | async-start | bytes 131072 | tf_op jit(solution)/shard_map/all_to_all | solution.py:506
  32.6 1.8 %collective-permute-start.8 = (bf16[128,768]{1,0:T(8,128)(2,1)}, bf16[128,768]{1,0:T(8,128)(2,1)S(1)}, u32[]{:S(2)}, u32[]{:S(2)}) collective-permute-start(bf16[128,768]{1,0:T(8,128)(2,1)} %get-tuple-element.48), channel_id=1, source_target_pairs={{0,8},{4,12},{8,16},{12,20},{16,24},{20,28},{24,0},{28,4},{1,9},{5... | collective-permute-start | bytes 589832 | tf_op jit(solution)/shard_map/ppermute | solution.py:441
  34.5 1.5 %collective-permute-start.9 = (bf16[128,768]{1,0:T(8,128)(2,1)}, bf16[128,768]{1,0:T(8,128)(2,1)S(1)}, u32[]{:S(2)}, u32[]{:S(2)}) collective-permute-start(bf16[128,768]{1,0:T(8,128)(2,1)} %copy-done.14), channel_id=1, source_target_pairs={{0,16},{4,20},{8,24},{12,28},{16,0},{20,4},{24,8},{28,12},{1,17},{... | collective-permute-start | bytes 589832 | tf_op jit(solution)/shard_map/ppermute | solution.py:441
  35.9 4.3 %all-to-all-done.mel_ref = bf16[32,8,128]{2,1,0:T(8,128)(2,1)S(1)} async-done(((bf16[32,8,128]{2,1,0:T(8,128)(2,1)}), bf16[32,8,128]{2,1,0:T(8,128)(2,1)S(1)}, u32[]{:S(2)}, u32[]{:S(2)}) %all-to-all-start) | async-done | bytes 65568 | tf_op jit(solution)/shard_map/all_to_all | solution.py:506
  40.2 1.3 %copy-done.22 = bf16[2304,256]{1,0:T(8,128)(2,1)S(1)} copy-done((bf16[2304,256]{1,0:T(8,128)(2,1)S(1)}, bf16[2304,256]{1,0:T(8,128)(2,1)}, u32[]{:S(2)}) %copy-start.22) | copy-done | bytes 1179672
  41.5 1.1 %copy-done.24 = bf16[128,2816]{1,0:T(8,128)(2,1)S(1)} copy-done((bf16[128,2816]{1,0:T(8,128)(2,1)S(1)}, bf16[128,2816]{1,0:T(8,128)(2,1)}, u32[]{:S(2)}) %copy-start.24) | copy-done | bytes 720920
  42.6 1.0 %copy-done.26 = bf16[288,512]{1,0:T(8,128)(2,1)S(1)} copy-done((bf16[288,512]{1,0:T(8,128)(2,1)S(1)}, bf16[288,512]{1,0:T(8,128)(2,1)}, u32[]{:S(2)}) %copy-start.26) | copy-done | bytes 294936
  43.6 0.8 copy-done.28
  44.4 5.6 %conv.1 = (bf16[64,1024]{1,0:T(8,128)(2,1)S(1)}, bf16[64,1024]{1,0:T(8,128)(2,1)S(1)}, bf16[64,1024]{1,0:T(8,128)(2,1)S(1)}, bf16[64,1024]{1,0:T(8,128)(2,1)S(1)}, bf16[4,1024,128]{2,1,0:T(8,128)(2,1)S(1)}) custom-call(bf16[32,8,128]{2,1,0:T(8,128)(2,1)S(1)} %all-to-all-done.mel_ref, bf16[128,2816]{1,0:T(8,128)(2,1)S(1)} %copy-done.24, ...), custom_call_target="tpu_custom_call" | custom-call | flops 8000000000 | bytes 4000000 | tf_op jit(solution)/shard_map/conv/pallas_call | solution.py:509
  50.1 0.6 collective-permute-start.10
  50.8 1.4 %collective-permute-start.5 = (bf16[64,1024]{1,0:T(8,128)(2,1)S(1)}, bf16[64,1024]{1,0:T(8,128)(2,1)S(1)}, u32[]{:S(2)}, u32[]{:S(2)}) collective-permute-start(bf16[64,1024]{1,0:T(8,128)(2,1)S(1)} %get-tuple-element.44), channel_id=1, source_target_pairs={{0,8},{4,12},{8,16},{12,20},{16,24},{20,28},{24,0},{28,4},{1,9},{5... | collective-permute-start | bytes 393224 | tf_op jit(solution)/shard_map/ppermute | solution.py:441
  52.9 2.3 %collective-permute-start.7 = (bf16[64,1024]{1,0:T(8,128)(2,1)S(1)}, bf16[64,1024]{1,0:T(8,128)(2,1)S(1)}, u32[]{:S(2)}, u32[]{:S(2)}) collective-permute-start(bf16[64,1024]{1,0:T(8,128)(2,1)S(1)} %get-tuple-element.46), channel_id=1, source_target_pairs={{0,24},{4,28},{8,0},{12,4},{16,8},{20,12},{24,16},{28,20},{1,25},{... | collective-permute-start | bytes 393224 | tf_op jit(solution)/shard_map/ppermute | solution.py:441
  55.2 2.7 %collective-permute-done.10.refs_7_ = bf16[128,768]{1,0:T(8,128)(2,1)S(1)} collective-permute-done((bf16[128,768]{1,0:T(8,128)(2,1)S(1)}, bf16[128,768]{1,0:T(8,128)(2,1)S(1)}, u32[]{:S(2)}, u32[]{:S(2)}) %collective-permute-start.10) | collective-permute-done | bytes 196640 | tf_op jit(solution)/shard_map/ppermute | solution.py:441
  57.9 2.9 %collective-permute-done.5.refs_1_ = bf16[64,1024]{1,0:T(8,128)(2,1)S(1)} collective-permute-done((bf16[64,1024]{1,0:T(8,128)(2,1)S(1)}, bf16[64,1024]{1,0:T(8,128)(2,1)S(1)}, u32[]{:S(2)}, u32[]{:S(2)}) %collective-permute-start.5) | collective-permute-done | bytes 131104 | tf_op jit(solution)/shard_map/ppermute | solution.py:441
  60.8 2.3 %collective-permute-done.7.refs_3_ = bf16[64,1024]{1,0:T(8,128)(2,1)S(1)} collective-permute-done((bf16[64,1024]{1,0:T(8,128)(2,1)S(1)}, bf16[64,1024]{1,0:T(8,128)(2,1)S(1)}, u32[]{:S(2)}, u32[]{:S(2)}) %collective-permute-start.7) | collective-permute-done | bytes 131104 | tf_op jit(solution)/shard_map/ppermute | solution.py:441
  63.1 1.9 %layer_norm.1 = (bf16[64,1024]{1,0:T(8,128)(2,1)S(1)}, bf16[64,1024]{1,0:T(8,128)(2,1)S(1)}, bf16[4,128,768]{2,1,0:T(8,128)(2,1)S(1)}) custom-call(s32[8]{0:T(128)S(1)} %copy-done.4, s32[8]{0:T(128)S(1)} %copy-done.5, s32[8]{0:T(128)S(1)} %copy-done.6, bf16[64,64]{1,0:T(8,128)(2,1)S(1)} %copy-done.2, s32[64,1]{1,0:T(8,128)S(1)} %copy-done.1, ...), custom_call_target="tpu_custom_call" | custom-call | flops 100000000 | bytes 1000000 | tf_op jit(solution)/shard_map/layer_norm/pallas_call | solution.py:535
  65.1 1.6 %collective-permute-start.13 = (bf16[64,1024]{1,0:T(8,128)(2,1)S(1)}, bf16[64,1024]{1,0:T(8,128)(2,1)S(1)}, u32[]{:S(2)}, u32[]{:S(2)}) collective-permute-start(bf16[64,1024]{1,0:T(8,128)(2,1)S(1)} %get-tuple-element.51.refs_0_), channel_id=1, source_target_pairs={{0,24},{4,28},{8,0},{12,4},{16,8},{20,12},{24,16},{28,20},{1,25},{... | collective-permute-start | bytes 393224 | tf_op jit(solution)/shard_map/ppermute | solution.py:441
  66.7 1.5 %collective-permute-start.12 = (bf16[64,1024]{1,0:T(8,128)(2,1)S(1)}, bf16[64,1024]{1,0:T(8,128)(2,1)S(1)}, u32[]{:S(2)}, u32[]{:S(2)}) collective-permute-start(bf16[64,1024]{1,0:T(8,128)(2,1)S(1)} %get-tuple-element.51.refs_0_), channel_id=1, source_target_pairs={{0,16},{4,20},{8,24},{12,28},{16,0},{20,4},{24,8},{28,12},{1,17},{... | collective-permute-start | bytes 393224 | tf_op jit(solution)/shard_map/ppermute | solution.py:441
  68.2 3.1 %collective-permute-done.13.refs_3_ = bf16[64,1024]{1,0:T(8,128)(2,1)S(1)} collective-permute-done((bf16[64,1024]{1,0:T(8,128)(2,1)S(1)}, bf16[64,1024]{1,0:T(8,128)(2,1)S(1)}, u32[]{:S(2)}, u32[]{:S(2)}) %collective-permute-start.13) | collective-permute-done | bytes 131104 | tf_op jit(solution)/shard_map/ppermute | solution.py:441
  71.3 0.7 collective-permute-start.16
  72.0 3.1 %collective-permute-done.12.refs_2_ = bf16[64,1024]{1,0:T(8,128)(2,1)S(1)} collective-permute-done((bf16[64,1024]{1,0:T(8,128)(2,1)S(1)}, bf16[64,1024]{1,0:T(8,128)(2,1)S(1)}, u32[]{:S(2)}, u32[]{:S(2)}) %collective-permute-start.12) | collective-permute-done | bytes 131104 | tf_op jit(solution)/shard_map/ppermute | solution.py:441
  75.1 4.2 %attention.1 = (bf16[64,256]{1,0:T(8,128)(2,1)S(1)}, bf16[64,256]{1,0:T(8,128)(2,1)S(1)}, bf16[64,256]{1,0:T(8,128)(2,1)S(1)}, bf16[64,256]{1,0:T(8,128)(2,1)S(1)}, bf16[8,1024,128]{2,1,0:T(8,128)(2,1)S(1)}) custom-call(s32[8]{0:T(128)S(1)} %copy-done.4, s32[8]{0:T(128)S(1)} %copy-done.5, s32[8]{0:T(128)S(1)} %copy-done.6, s32[1,64]{1,0:T(1,128)S(1)} %copy-done.8, ...), custom_call_target="tpu_custom_call" | custom-call | flops 1000000000 | bytes 2000000 | tf_op jit(solution)/shard_map/attention/pallas_call | solution.py:550
  79.3 0.7 collective-permute-start.17
  79.9 5.8 %collective-permute-start.18 = (bf16[64,256]{1,0:T(8,128)(2,1)S(1)}, bf16[64,256]{1,0:T(8,128)(2,1)S(1)}, u32[]{:S(2)}, u32[]{:S(2)}) collective-permute-start(bf16[64,256]{1,0:T(8,128)(2,1)S(1)} %get-tuple-element.57), channel_id=1, source_target_pairs={{0,3},{1,11},{2,19},{3,27},{4,7},{5,15},{6,23},{7,31},{8,0},{9,8},... | collective-permute-start | bytes 98312 | tf_op jit(solution)/shard_map/ppermute | solution.py:453
  85.8 2.0 %collective-permute-start.20 = (bf16[64,256]{1,0:T(8,128)(2,1)S(1)}, bf16[64,256]{1,0:T(8,128)(2,1)S(1)}, u32[]{:S(2)}, u32[]{:S(2)}) collective-permute-start(bf16[64,256]{1,0:T(8,128)(2,1)S(1)} %get-tuple-element.59), channel_id=1, source_target_pairs={{0,1},{1,9},{2,17},{3,25},{4,5},{5,13},{6,21},{7,29},{8,2},{9,10},... | collective-permute-start | bytes 98312 | tf_op jit(solution)/shard_map/ppermute | solution.py:453
  87.8 1.9 %collective-permute-done.19.refs_2_ = bf16[64,256]{1,0:T(8,128)(2,1)S(1)} collective-permute-done((bf16[64,256]{1,0:T(8,128)(2,1)S(1)}, bf16[64,256]{1,0:T(8,128)(2,1)S(1)}, u32[]{:S(2)}, u32[]{:S(2)}) %collective-permute-start.19) | collective-permute-done | bytes 32800 | tf_op jit(solution)/shard_map/ppermute | solution.py:453
  89.7 1.4 %collective-permute-done.20.refs_3_ = bf16[64,256]{1,0:T(8,128)(2,1)S(1)} collective-permute-done((bf16[64,256]{1,0:T(8,128)(2,1)S(1)}, bf16[64,256]{1,0:T(8,128)(2,1)S(1)}, u32[]{:S(2)}, u32[]{:S(2)}) %collective-permute-start.20) | collective-permute-done | bytes 32800 | tf_op jit(solution)/shard_map/ppermute | solution.py:453
  91.1 1.9 %output.1 = (bf16[64,1024]{1,0:T(8,128)(2,1)}, bf16[64,1024]{1,0:T(8,128)(2,1)}) custom-call(s32[8]{0:T(128)S(1)} %copy-done.4, s32[8]{0:T(128)S(1)} %copy-done.5, s32[8]{0:T(128)S(1)} %copy-done.6, bf16[64,64]{1,0:T(8,128)(2,1)S(1)} %copy-done.2, s32[64,1]{1,0:T(8,128)S(1)} %copy-done.1, bf16[8,1024,128]{2,1,0:T(8,128)(2,1)S(1)} %get-tuple-element.54.weights_ref, ...), custom_call_target="tpu_custom_call" | custom-call | flops 100000000 | bytes 3000000 | tf_op jit(solution)/shard_map/output/pallas_call | solution.py:565
  (61 shorter events, 1.9 us)
Async XLA Ops:
  0.6 39.6 %collective-permute-start.1 = (bf16[640,1024]{1,0:T(8,128)(2,1)}, bf16[640,1024]{1,0:T(8,128)(2,1)S(1)}, u32[]{:S(2)}, u32[]{:S(2)}) collective-permute-start(bf16[640,1024]{1,0:T(8,128)(2,1)} %refs_0_.3), channel_id=1, source_target_pairs={{0,4},{4,0},{8,12},{12,8},{16,20},{20,16},{24,28},{28,24},{1,5},{5... | collective-permute-start | bytes 3932168 | tf_op jit(solution)/shard_map/ppermute | solution.py:445
  1.9 7.1 %collective-permute-start = (f32[8,384]{1,0:T(8,128)S(1)}, f32[8,384]{1,0:T(8,128)S(1)}, u32[]{:S(2)}, u32[]{:S(2)}) collective-permute-start(f32[8,384]{1,0:T(8,128)S(1)} %slice.3), channel_id=1, source_target_pairs={{0,1},{1,2},{2,3},{3,4},{4,5},{5,6},{6,7},{7,8},{8,9},{9,10},{10,1... | collective-permute-start | bytes 36872 | tf_op jit(solution)/shard_map/ppermute | solution.py:437
  6.3 1.1 %copy-start = (bf16[128,3072]{1,0:T(8,128)(2,1)S(1)}, bf16[128,3072]{1,0:T(8,128)(2,1)}, u32[]{:S(2)}) copy-start(bf16[128,3072]{1,0:T(8,128)(2,1)} %qkv_ref.1) | copy-start | bytes 2359300
  9.0 20.9 %copy-start.14 = (bf16[128,768]{1,0:T(8,128)(2,1)}, bf16[128,768]{1,0:T(8,128)(2,1)S(1)}, u32[]{:S(2)}) copy-start(bf16[128,768]{1,0:T(8,128)(2,1)S(1)} %get-tuple-element.49) | copy-start | bytes 589828
  9.0 25.5 %collective-permute-start.4 = (bf16[1024,128]{1,0:T(8,128)(2,1)}, bf16[1024,128]{1,0:T(8,128)(2,1)}, u32[]{:S(2)}, u32[]{:S(2)}) collective-permute-start(bf16[1024,128]{1,0:T(8,128)(2,1)} %refs_2_.1), channel_id=1, source_target_pairs={{0,24},{4,28},{8,0},{12,4},{16,8},{20,12},{24,16},{28,20},{1,25},{... | collective-permute-start | bytes 786440 | tf_op jit(solution)/shard_map/ppermute | solution.py:441
  13.0 27.2 %collective-permute-start.3 = (bf16[1024,128]{1,0:T(8,128)(2,1)}, bf16[1024,128]{1,0:T(8,128)(2,1)}, u32[]{:S(2)}, u32[]{:S(2)}) collective-permute-start(bf16[1024,128]{1,0:T(8,128)(2,1)} %refs_2_.1), channel_id=1, source_target_pairs={{0,16},{4,20},{8,24},{12,28},{16,0},{20,4},{24,8},{28,12},{1,17},{... | collective-permute-start | bytes 786440 | tf_op jit(solution)/shard_map/ppermute | solution.py:441
  13.5 26.7 %collective-permute-start.2 = (bf16[1024,128]{1,0:T(8,128)(2,1)}, bf16[1024,128]{1,0:T(8,128)(2,1)}, u32[]{:S(2)}, u32[]{:S(2)}) collective-permute-start(bf16[1024,128]{1,0:T(8,128)(2,1)} %refs_2_.1), channel_id=1, source_target_pairs={{0,8},{4,12},{8,16},{12,20},{16,24},{20,28},{24,0},{28,4},{1,9},{5... | collective-permute-start | bytes 786440 | tf_op jit(solution)/shard_map/ppermute | solution.py:441
  15.7 0.9 copy-start.7
  16.6 1.3 %copy-start.10 = (bf16[2304,256]{1,0:T(8,128)(2,1)S(1)}, bf16[2304,256]{1,0:T(8,128)(2,1)}, u32[]{:S(2)}) copy-start(bf16[2304,256]{1,0:T(8,128)(2,1)} %refs_0_.2) | copy-start | bytes 3538948
  18.6 1.2 %copy-start.16 = (f32[512,512]{1,0:T(8,128)S(1)}, f32[512,512]{1,0:T(8,128)}, u32[]{:S(2)}) copy-start(f32[512,512]{1,0:T(8,128)} %constant.18.clone.table_ref) | copy-start | bytes 3145732
  19.8 1.0 %copy-start.17 = (bf16[512,512]{1,0:T(8,128)(2,1)S(1)}, bf16[512,512]{1,0:T(8,128)(2,1)}, u32[]{:S(2)}) copy-start(bf16[512,512]{1,0:T(8,128)(2,1)} %constant.20.clone.select_ref) | copy-start | bytes 1572868
  20.8 1.0 %copy-start.18 = (bf16[288,512]{1,0:T(8,128)(2,1)S(1)}, bf16[288,512]{1,0:T(8,128)(2,1)}, u32[]{:S(2)}) copy-start(bf16[288,512]{1,0:T(8,128)(2,1)} %constant.16.clone.refs_1_) | copy-start | bytes 884740
  21.8 0.9 copy-start.19
  22.7 0.8 copy-start.20
  23.5 16.7 %copy-start.9 = (bf16[640,1024]{1,0:T(8,128)(2,1)S(1)}, bf16[640,1024]{1,0:T(8,128)(2,1)}, u32[]{:S(2)}) copy-start(bf16[640,1024]{1,0:T(8,128)(2,1)} %refs_0_.3) | copy-start | bytes 3932164
  23.5 16.7 %copy-start.11 = (bf16[1024,128]{1,0:T(8,128)(2,1)S(1)}, bf16[1024,128]{1,0:T(8,128)(2,1)}, u32[]{:S(2)}) copy-start(bf16[1024,128]{1,0:T(8,128)(2,1)} %refs_2_.1) | copy-start | bytes 786436
  27.2 1.1 %copy-start.21 = (bf16[2304,256]{1,0:T(8,128)(2,1)}, bf16[2304,256]{1,0:T(8,128)(2,1)S(1)}, u32[]{:S(2)}) copy-start(bf16[2304,256]{1,0:T(8,128)(2,1)S(1)} %get-tuple-element.39.conv2) | copy-start | bytes 3538948
  28.2 0.9 copy-start.23
  29.1 0.7 copy-start.25
  29.8 4.6 %copy-start.27 = (bf16[128,256]{1,0:T(8,128)(2,1)}, bf16[128,256]{1,0:T(8,128)(2,1)S(1)}, u32[]{:S(2)}) copy-start(bf16[128,256]{1,0:T(8,128)(2,1)S(1)} %get-tuple-element.41.shift_ref) | copy-start | bytes 196612
  29.8 10.3 %all-to-all-start = ((bf16[32,8,128]{2,1,0:T(8,128)(2,1)}), bf16[32,8,128]{2,1,0:T(8,128)(2,1)S(1)}, u32[]{:S(2)}, u32[]{:S(2)}) async-start(bf16[32,8,128]{2,1,0:T(8,128)(2,1)} %get-tuple-element.37), calls=%async_computation | async-start | bytes 131072 | tf_op jit(solution)/shard_map/all_to_all | solution.py:506
  32.6 19.6 %collective-permute-start.8 = (bf16[128,768]{1,0:T(8,128)(2,1)}, bf16[128,768]{1,0:T(8,128)(2,1)S(1)}, u32[]{:S(2)}, u32[]{:S(2)}) collective-permute-start(bf16[128,768]{1,0:T(8,128)(2,1)} %get-tuple-element.48), channel_id=1, source_target_pairs={{0,8},{4,12},{8,16},{12,20},{16,24},{20,28},{24,0},{28,4},{1,9},{5... | collective-permute-start | bytes 589832 | tf_op jit(solution)/shard_map/ppermute | solution.py:441
  34.5 18.4 %collective-permute-start.9 = (bf16[128,768]{1,0:T(8,128)(2,1)}, bf16[128,768]{1,0:T(8,128)(2,1)S(1)}, u32[]{:S(2)}, u32[]{:S(2)}) collective-permute-start(bf16[128,768]{1,0:T(8,128)(2,1)} %copy-done.14), channel_id=1, source_target_pairs={{0,16},{4,20},{8,24},{12,28},{16,0},{20,4},{24,8},{28,12},{1,17},{... | collective-permute-start | bytes 589832 | tf_op jit(solution)/shard_map/ppermute | solution.py:441
  40.2 1.3 %copy-start.22 = (bf16[2304,256]{1,0:T(8,128)(2,1)S(1)}, bf16[2304,256]{1,0:T(8,128)(2,1)}, u32[]{:S(2)}) copy-start(bf16[2304,256]{1,0:T(8,128)(2,1)} %copy-done.21) | copy-start | bytes 3538948
  41.5 1.1 %copy-start.24 = (bf16[128,2816]{1,0:T(8,128)(2,1)S(1)}, bf16[128,2816]{1,0:T(8,128)(2,1)}, u32[]{:S(2)}) copy-start(bf16[128,2816]{1,0:T(8,128)(2,1)} %copy-done.23) | copy-start | bytes 2162692
  42.6 1.0 %copy-start.26 = (bf16[288,512]{1,0:T(8,128)(2,1)S(1)}, bf16[288,512]{1,0:T(8,128)(2,1)}, u32[]{:S(2)}) copy-start(bf16[288,512]{1,0:T(8,128)(2,1)} %copy-done.25) | copy-start | bytes 884740
  43.6 0.8 copy-start.28
  44.4 5.7 %copy-start.13 = (bf16[128,768]{1,0:T(8,128)(2,1)S(1)}, bf16[128,768]{1,0:T(8,128)(2,1)}, u32[]{:S(2)}) copy-start(bf16[128,768]{1,0:T(8,128)(2,1)} %copy-done.12) | copy-start | bytes 589828
  44.4 18.6 %copy-start.1 = (s32[64,1]{1,0:T(8,128)S(1)}, s32[64,1]{1,0:T(8,128)}, u32[]{:S(2)}) copy-start(s32[64,1]{1,0:T(8,128)} %constant.21.clone.sample_ref) | copy-start | bytes 772
  44.4 18.6 %copy-start.2 = (bf16[64,64]{1,0:T(8,128)(2,1)S(1)}, bf16[64,64]{1,0:T(8,128)(2,1)}, u32[]{:S(2)}) copy-start(bf16[64,64]{1,0:T(8,128)(2,1)} %constant.23.clone.frames_ref) | copy-start | bytes 24580
  44.4 18.6 %copy-start.4 = (s32[8]{0:T(128)S(1)}, s32[8]{0:T(128)}, u32[]{:S(2)}) copy-start(s32[8]{0:T(128)} %slots_ref.7) | copy-start | bytes 100
  44.4 18.6 %copy-start.5 = (s32[8]{0:T(128)S(1)}, s32[8]{0:T(128)}, u32[]{:S(2)}) copy-start(s32[8]{0:T(128)} %starts_ref.5) | copy-start | bytes 100
  44.4 18.6 %copy-start.6 = (s32[8]{0:T(128)S(1)}, s32[8]{0:T(128)}, u32[]{:S(2)}) copy-start(s32[8]{0:T(128)} %lengths_ref.5) | copy-start | bytes 100
  50.0 25.0 %copy-start.8 = (s32[1,64]{1,0:T(1,128)S(1)}, s32[1,64]{1,0:T(1,128)}, u32[]{:S(2)}) copy-start(s32[1,64]{1,0:T(1,128)} %constant.22.clone.sample_ref) | copy-start | bytes 772
  50.0 25.0 %collective-permute-start.15 = (bf16[4,1024,128]{2,1,0:T(8,128)(2,1)S(1)}, bf16[4,1024,128]{2,1,0:T(8,128)(2,1)S(1)}, u32[]{:S(2)}, u32[]{:S(2)}) collective-permute-start(bf16[4,1024,128]{2,1,0:T(8,128)(2,1)S(1)} %get-tuple-element.53.refs_6_), channel_id=1, source_target_pairs={{0,4},{4,0},{8,12},{12,8},{16,20},{20,16},{24,28},{28,24},{1,5},{5... | collective-permute-start | bytes 3145736 | tf_op jit(solution)/shard_map/ppermute | solution.py:445
  50.1 7.8 %collective-permute-start.10 = (bf16[128,768]{1,0:T(8,128)(2,1)S(1)}, bf16[128,768]{1,0:T(8,128)(2,1)S(1)}, u32[]{:S(2)}, u32[]{:S(2)}) collective-permute-start(bf16[128,768]{1,0:T(8,128)(2,1)S(1)} %copy-done.13), channel_id=1, source_target_pairs={{0,24},{4,28},{8,0},{12,4},{16,8},{20,12},{24,16},{28,20},{1,25},{... | collective-permute-start | bytes 589832 | tf_op jit(solution)/shard_map/ppermute | solution.py:441
  50.8 10.0 %collective-permute-start.5 = (bf16[64,1024]{1,0:T(8,128)(2,1)S(1)}, bf16[64,1024]{1,0:T(8,128)(2,1)S(1)}, u32[]{:S(2)}, u32[]{:S(2)}) collective-permute-start(bf16[64,1024]{1,0:T(8,128)(2,1)S(1)} %get-tuple-element.44), channel_id=1, source_target_pairs={{0,8},{4,12},{8,16},{12,20},{16,24},{20,28},{24,0},{28,4},{1,9},{5... | collective-permute-start | bytes 393224 | tf_op jit(solution)/shard_map/ppermute | solution.py:441
  52.2 8.6 %collective-permute-start.6 = (bf16[64,1024]{1,0:T(8,128)(2,1)S(1)}, bf16[64,1024]{1,0:T(8,128)(2,1)S(1)}, u32[]{:S(2)}, u32[]{:S(2)}) collective-permute-start(bf16[64,1024]{1,0:T(8,128)(2,1)S(1)} %get-tuple-element.45), channel_id=1, source_target_pairs={{0,16},{4,20},{8,24},{12,28},{16,0},{20,4},{24,8},{28,12},{1,17},{... | collective-permute-start | bytes 393224 | tf_op jit(solution)/shard_map/ppermute | solution.py:441
  52.9 10.2 %collective-permute-start.7 = (bf16[64,1024]{1,0:T(8,128)(2,1)S(1)}, bf16[64,1024]{1,0:T(8,128)(2,1)S(1)}, u32[]{:S(2)}, u32[]{:S(2)}) collective-permute-start(bf16[64,1024]{1,0:T(8,128)(2,1)S(1)} %get-tuple-element.46), channel_id=1, source_target_pairs={{0,24},{4,28},{8,0},{12,4},{16,8},{20,12},{24,16},{28,20},{1,25},{... | collective-permute-start | bytes 393224 | tf_op jit(solution)/shard_map/ppermute | solution.py:441
  65.0 10.0 %collective-permute-start.14 = (bf16[4,128,768]{2,1,0:T(8,128)(2,1)S(1)}, bf16[4,128,768]{2,1,0:T(8,128)(2,1)S(1)}, u32[]{:S(2)}, u32[]{:S(2)}) collective-permute-start(bf16[4,128,768]{2,1,0:T(8,128)(2,1)S(1)} %get-tuple-element.52.refs_4_), channel_id=1, source_target_pairs={{0,4},{4,0},{8,12},{12,8},{16,20},{20,16},{24,28},{28,24},{1,5},{5... | collective-permute-start | bytes 2359304 | tf_op jit(solution)/shard_map/ppermute | solution.py:445
  65.1 6.2 %collective-permute-start.13 = (bf16[64,1024]{1,0:T(8,128)(2,1)S(1)}, bf16[64,1024]{1,0:T(8,128)(2,1)S(1)}, u32[]{:S(2)}, u32[]{:S(2)}) collective-permute-start(bf16[64,1024]{1,0:T(8,128)(2,1)S(1)} %get-tuple-element.51.refs_0_), channel_id=1, source_target_pairs={{0,24},{4,28},{8,0},{12,4},{16,8},{20,12},{24,16},{28,20},{1,25},{... | collective-permute-start | bytes 393224 | tf_op jit(solution)/shard_map/ppermute | solution.py:441
  66.7 8.4 %collective-permute-start.12 = (bf16[64,1024]{1,0:T(8,128)(2,1)S(1)}, bf16[64,1024]{1,0:T(8,128)(2,1)S(1)}, u32[]{:S(2)}, u32[]{:S(2)}) collective-permute-start(bf16[64,1024]{1,0:T(8,128)(2,1)S(1)} %get-tuple-element.51.refs_0_), channel_id=1, source_target_pairs={{0,16},{4,20},{8,24},{12,28},{16,0},{20,4},{24,8},{28,12},{1,17},{... | collective-permute-start | bytes 393224 | tf_op jit(solution)/shard_map/ppermute | solution.py:441
  68.2 6.9 %collective-permute-start.11 = (bf16[64,1024]{1,0:T(8,128)(2,1)S(1)}, bf16[64,1024]{1,0:T(8,128)(2,1)S(1)}, u32[]{:S(2)}, u32[]{:S(2)}) collective-permute-start(bf16[64,1024]{1,0:T(8,128)(2,1)S(1)} %get-tuple-element.51.refs_0_), channel_id=1, source_target_pairs={{0,8},{4,12},{8,16},{12,20},{16,24},{20,28},{24,0},{28,4},{1,9},{5... | collective-permute-start | bytes 393224 | tf_op jit(solution)/shard_map/ppermute | solution.py:441
  71.3 16.5 %collective-permute-start.16 = (bf16[64,1024]{1,0:T(8,128)(2,1)S(1)}, bf16[64,1024]{1,0:T(8,128)(2,1)S(1)}, u32[]{:S(2)}, u32[]{:S(2)}) collective-permute-start(bf16[64,1024]{1,0:T(8,128)(2,1)S(1)} %get-tuple-element.55), channel_id=1, source_target_pairs={{0,0},{1,8},{2,16},{3,24},{4,4},{5,12},{6,20},{7,28},{8,1},{9,9},{... | collective-permute-start | bytes 393224 | tf_op jit(solution)/shard_map/ppermute | solution.py:453
  79.3 8.5 %collective-permute-start.17 = (bf16[64,256]{1,0:T(8,128)(2,1)S(1)}, bf16[64,256]{1,0:T(8,128)(2,1)S(1)}, u32[]{:S(2)}, u32[]{:S(2)}) collective-permute-start(bf16[64,256]{1,0:T(8,128)(2,1)S(1)} %get-tuple-element.56), channel_id=1, source_target_pairs={{0,0},{1,8},{2,16},{3,24},{4,4},{5,12},{6,20},{7,28},{8,1},{9,9},{... | collective-permute-start | bytes 98312 | tf_op jit(solution)/shard_map/ppermute | solution.py:453
  79.9 7.8 %collective-permute-start.18 = (bf16[64,256]{1,0:T(8,128)(2,1)S(1)}, bf16[64,256]{1,0:T(8,128)(2,1)S(1)}, u32[]{:S(2)}, u32[]{:S(2)}) collective-permute-start(bf16[64,256]{1,0:T(8,128)(2,1)S(1)} %get-tuple-element.57), channel_id=1, source_target_pairs={{0,3},{1,11},{2,19},{3,27},{4,7},{5,15},{6,23},{7,31},{8,0},{9,8},... | collective-permute-start | bytes 98312 | tf_op jit(solution)/shard_map/ppermute | solution.py:453
  85.8 3.9 %collective-permute-start.19 = (bf16[64,256]{1,0:T(8,128)(2,1)S(1)}, bf16[64,256]{1,0:T(8,128)(2,1)S(1)}, u32[]{:S(2)}, u32[]{:S(2)}) collective-permute-start(bf16[64,256]{1,0:T(8,128)(2,1)S(1)} %get-tuple-element.58), channel_id=1, source_target_pairs={{0,2},{1,10},{2,18},{3,26},{4,6},{5,14},{6,22},{7,30},{8,3},{9,11}... | collective-permute-start | bytes 98312 | tf_op jit(solution)/shard_map/ppermute | solution.py:453
  85.8 5.3 %collective-permute-start.20 = (bf16[64,256]{1,0:T(8,128)(2,1)S(1)}, bf16[64,256]{1,0:T(8,128)(2,1)S(1)}, u32[]{:S(2)}, u32[]{:S(2)}) collective-permute-start(bf16[64,256]{1,0:T(8,128)(2,1)S(1)} %get-tuple-element.59), channel_id=1, source_target_pairs={{0,1},{1,9},{2,17},{3,25},{4,5},{5,13},{6,21},{7,29},{8,2},{9,10},... | collective-permute-start | bytes 98312 | tf_op jit(solution)/shard_map/ppermute | solution.py:453
  (3 other events, 2.0 us)
